TPU v7x, 128 devices: a whole 4x4x4 slice. The times are simulated.
128 devices in a mesh: lon: 16 (over z, y_lo, core), lat: 8 (over x, y_hi).
Axes of the slice: x: 4, y: 4 (y_hi: 2, y_lo: 2; y = y_hi * 2 + y_lo), z: 4, core: 2. Of those that a mesh axis runs over, the one named last changes fastest.
Arguments:
- east_velocity: float32 [16, 1216, 4096], P(None, 'lat', 'lon'), may hold values from -3 to 3
- north_velocity: float32 [16, 1216, 4096], P(None, 'lat', 'lon'), may hold values from -3 to 3
- heat_anomaly: float32 [16, 1216, 4096], P(None, 'lat', 'lon'), may hold values from -6 to 6
- haline_anomaly: float32 [16, 1216, 4096], P(None, 'lat', 'lon'), may hold values from -6 to 6
- spacing_lengths: float32 [6, 1216, 4096], P(None, 'lat', 'lon'), may hold values from 0.5 to 2
- planetary_spin: float32 [2, 1216, 4096], P(None, 'lat', 'lon'), may hold values from -1.5 to 1.5
- ocean_layer_number: int32 [1216, 4096], P('lat', 'lon'), may hold values from 0 to 16
- seam_partner_index: int32 [4096], replicated, may hold values from 0 to 4095, as said below
Outputs:
- stepped_zonal_speed: float32 [16, 1216, 4096], P(None, 'lat', 'lon')
- meridional_next: float32 [16, 1216, 4096], P(None, 'lat', 'lon')
- stepped_heat: float32 [16, 1216, 4096], P(None, 'lat', 'lon')
Inputs may be any that keep to these rules, and one draw needn't show every extreme that they name: `seam_partner_index`: for a column in longitude block b of 256 columns, its partner lies in block 15 - b; every column is the partner of exactly one column.
All inputs are finite; a program needn't handle non-finite values.
Results may differ from a plain program's by a relative error of at most 0.0003.
Values sent between devices are 32-bit elements; how exact they have to be, the bound alone decides.
No kernel may reach another device: no remote copies, remote signals or barrier semaphores. Data moves between devices by JAX's collectives and lax.ppermute only.
A program may use at most 192 MiB of HBM per device.

v0:
```python
import jax
import jax.numpy as jnp
from jax import lax
from jax.experimental import pallas as pl
from jax.experimental.pallas import tpu as pltpu
from jax.sharding import PartitionSpec as P

LANES = 128
TILE = 8

step_duration = 0.25
viscosity = 0.05
diffusivity = 0.3
expansion_coefficient = 0.6
haline_contraction = 0.8
gravity = 0.1

NEAR, FAR, DENS, ZONAL, MERID = 0, 1, 2, 3, 4
E1V_AT, E2V_AT, WET_AT = 0, 1, 2
E1U_LANE, E2U_LANE, WET_LANE = 80, 81, 82


def density_of(salinity, heat):
    return haline_contraction * salinity - expansion_coefficient * heat


def inverse_of(x):
    r = pl.reciprocal(x, approx=True)
    return r * (2.0 - x * r)


def row_pack(t_lo, t_hi, s_lo, s_hi, u_lo, u_hi, v_lo, v_hi, e_lo, e_hi, n_lo, n_hi, first, second):
    levels = t_lo.shape[0]
    even = lax.rem(lax.axis_index("lat"), 2) == 0

    def put(slot, high, low):
        rows = pl.ds(slot * levels, levels)
        first[rows] = jnp.where(even, high, low)
        second[rows] = jnp.where(even, low, high)

    near_hi, near_lo = t_hi[:, 7, :], t_lo[:, 0, :]
    put(NEAR, near_hi, near_lo)
    put(FAR, t_hi[:, 6, :], t_lo[:, 1, :])
    put(DENS, density_of(s_hi[:, 7, :], near_hi), density_of(s_lo[:, 0, :], near_lo))
    put(ZONAL, u_hi[:, 7, :], u_lo[:, 0, :])
    put(MERID, v_hi[:, 7, :], v_lo[:, 0, :])
    base = 5 * levels
    high = jnp.concatenate([e_hi[4, 7:8], e_hi[5, 7:8], n_hi[7:8].astype(jnp.float32), jnp.zeros((5, e_hi.shape[2]), jnp.float32)], axis=0)
    low = jnp.concatenate([e_lo[4, 0:1], e_lo[5, 0:1], n_lo[0:1].astype(jnp.float32), jnp.zeros((5, e_lo.shape[2]), jnp.float32)], axis=0)
    first[base : base + 8] = jnp.where(even, high, low)
    second[base : base + 8] = jnp.where(even, low, high)


def vertical_span(x):
    return jnp.concatenate([x[1:], x[-1:]], axis=0) - jnp.concatenate([x[:1], x[:-1]], axis=0)


def column_pack(group, t, s, u, v, e, n, mine1, mine2, got1, got2, seam, east_out, west_out, north_out, south_out):
    levels = t.shape[0] * pl.num_programs(0)
    rows = t.shape[1]
    cols = t.shape[2]
    lat, lon = lax.axis_index("lat"), lax.axis_index("lon")
    lats, lons = lax.axis_size("lat"), lax.axis_size("lon")
    even = lax.rem(lat, 2) == 0
    step = pl.program_id(0)
    lane = lax.broadcasted_iota(jnp.int32, (rows, LANES), 1)

    @pl.when(step == 0)
    def _():
        is_top = lat == lats - 1
        is_bottom = lat == 0
        north_rows = got1.shape[0]
        for h in range(cols // LANES):
            span = slice(h * LANES, (h + 1) * LANES)
            pick = seam[pl.ds(lon * (cols // LANES) + h, 1), :] - (lons - 1 - lon) * cols
            pick = jnp.where(is_top, pick, lax.broadcasted_iota(jnp.int32, (1, LANES), 1) + h * LANES)
            pick = jnp.broadcast_to(pick, (TILE, LANES))
            inner = jnp.bitwise_and(pick, LANES - 1)
            for row in range(0, north_rows, TILE):
                total = None
                for g in range(cols // LANES):
                    piece = slice(g * LANES, (g + 1) * LANES)
                    source = jnp.where(even, got1[row : row + TILE, piece], got2[row : row + TILE, piece])
                    taken = jnp.take_along_axis(source, inner, axis=1, mode="promise_in_bounds")
                    taken = jnp.where(pick >= g * LANES, taken, 0.0) if g == 0 else taken
                    total = taken if total is None else jnp.where(pick >= g * LANES, taken, total)
                if ZONAL * levels <= row < (MERID + 1) * levels:
                    total = jnp.where(is_top, -total, total)
                north_out[row : row + TILE, span] = total
        def south(slot):
            part = slice(slot * levels, (slot + 1) * levels)
            return jnp.where(is_bottom, 0.0, jnp.where(even, got2[part], got1[part]))

        def own(slot):
            part = slice(slot * levels, (slot + 1) * levels)
            return jnp.where(even, mine2[part], mine1[part])

        tail = slice(5 * levels, 5 * levels + 8)
        coef = jnp.where(even, got2[tail], got1[tail])
        own_wet = jnp.where(even, mine2[tail], mine1[tail])[WET_AT : WET_AT + 1]
        e1v = jnp.where(is_bottom, 1.0, coef[E1V_AT : E1V_AT + 1])
        e2v = jnp.where(is_bottom, 1.0, coef[E2V_AT : E2V_AT + 1])
        wet = jnp.where(is_bottom, 0.0, coef[WET_AT : WET_AT + 1])
        t_near, t_far, d_near, v_near = south(NEAR), south(FAR), south(DENS), south(MERID)
        t_own, t_next, d_own = own(NEAR), own(FAR), own(DENS)
        t_sum = t_near + t_own
        adv = (e1v / 12.0) * v_near * (7.0 * t_sum - (t_far + t_next))
        d_span = vertical_span(d_near + d_own)
        tilt = (d_own - d_near) * d_span * vertical_span(t_sum) / (d_span * d_span + 16.0)
        iso = (diffusivity * e1v / e2v) * (t_own - t_near - tilt)
        level = lax.broadcasted_iota(jnp.int32, (levels, cols), 0).astype(jnp.float32)
        flux = jnp.where(level < jnp.minimum(wet, own_wet), iso - adv, 0.0)
        south_out[0:levels] = t_near
        south_out[levels : 2 * levels] = flux
        south_out[2 * levels : 3 * levels] = south(ZONAL)
        south_out[3 * levels : 4 * levels] = v_near

        n_f = n[...].astype(jnp.float32)
        last = slice(cols - LANES, cols)
        hi = jnp.where(lane == E1U_LANE, pltpu.roll(e[2, :, last], (E1U_LANE + 1) % LANES, 1), 0.0)
        hi = jnp.where(lane == E2U_LANE, pltpu.roll(e[3, :, last], (E2U_LANE + 1) % LANES, 1), hi)
        hi = jnp.where(lane == WET_LANE, pltpu.roll(n_f[:, last], (WET_LANE + 1) % LANES, 1), hi)
        east_out[0:rows] = hi
        west_out[8 : rows + 8] = jnp.where(lane == WET_LANE, pltpu.roll(n_f[:, :LANES], WET_LANE, 1), 0.0)
        sub16 = lax.broadcasted_iota(jnp.int32, (levels, LANES), 0)
        lane16 = lax.broadcasted_iota(jnp.int32, (levels, LANES), 1)
        u_corner = jnp.broadcast_to(north_out[ZONAL * levels : (ZONAL + 1) * levels, cols - 1 : cols], (levels, LANES))
        u_row = jnp.sum(jnp.where(lane16 == sub16 + ZONAL * levels, u_corner, 0.0), axis=0, keepdims=True)
        v_corner = jnp.broadcast_to(v_near[:, 0:1], (levels, LANES))
        v_row = jnp.sum(jnp.where(lane16 == sub16 + MERID * levels, v_corner, 0.0), axis=0, keepdims=True)
        east_out[rows : rows + 8] = jnp.broadcast_to(u_row, (8, LANES))
        west_out[0:8] = jnp.broadcast_to(v_row, (8, LANES))

    first = slice(0, LANES)
    last = slice(cols - LANES, cols)
    hi = east_out[0:rows]
    lo = west_out[8 : rows + 8]
    for kk in range(group):
        k = step * group + kk
        t_hi, t_lo = t[kk, :, last], t[kk, :, first]
        d_hi, d_lo = density_of(s[kk, :, last], t_hi), density_of(s[kk, :, first], t_lo)
        parts = (
            (NEAR, t_hi, 127, t_lo, 0),
            (FAR, t_hi, 126, t_lo, 1),
            (DENS, d_hi, 127, d_lo, 0),
            (ZONAL, u[kk, :, last], 127, u[kk, :, first], 0),
            (MERID, v[kk, :, last], 127, v[kk, :, first], 0),
        )
        for slot, x_hi, at_hi, x_lo, at_lo in parts:
            place = slot * levels + k
            here = lane == place
            hi = jnp.where(here, pltpu.roll(x_hi, lax.rem(place + (2 * LANES - at_hi), LANES), 1), hi)
            lo = jnp.where(here, pltpu.roll(x_lo, lax.rem(place + (2 * LANES - at_lo), LANES), 1), lo)
    east_out[0:rows] = hi
    west_out[8 : rows + 8] = lo


def step_kernel(
    chunks,
    t_hbm, s_hbm, u_hbm, v_hbm, e_hbm, f_hbm, n_hbm, north, south, own_west, from_east, from_west,
    u_out, v_out, t_out,
    t_s, s_s, u_s, v_s, d_s, g_s, far_s, ue_s, uw_s, ve_s, vw_s,
    e_s, f_s, n_s, nf_s, uo_s, vo_s, to_s, shift_s, in_sem, flat_sem, out_sem,
):
    levels, rows, cols = t_hbm.shape
    tiles = rows // TILE
    halves = cols // LANES
    starts = [sum(chunks[:c]) for c in range(len(chunks))]

    def load(c, field, h):
        hbm, vmem = ((t_hbm, t_s), (s_hbm, s_s), (u_hbm, u_s), (v_hbm, v_s))[field]
        span = pl.ds(starts[c] * TILE, chunks[c] * TILE)
        held = pl.ds(starts[c] * TILE + TILE, chunks[c] * TILE)
        return pltpu.make_async_copy(
            hbm.at[:, span, pl.ds(h * LANES, LANES)], vmem.at[h, :, held, :], in_sem.at[c, field, h]
        )

    def store(c, field):
        vmem, hbm = ((uo_s, u_out), (vo_s, v_out), (to_s, t_out))[field]
        span = pl.ds(starts[c] * TILE, chunks[c] * TILE)
        return pltpu.make_async_copy(vmem.at[:, span, :], hbm.at[:, span, :], out_sem.at[c, field])

    flat = [
        pltpu.make_async_copy(hbm, vmem, flat_sem.at[i])
        for i, (hbm, vmem) in enumerate(((e_hbm, e_s), (f_hbm, f_s), (n_hbm, n_s)))
    ]
    flat[2].start()
    for field in range(4):
        for h in range(halves):
            load(0, field, h).start()
    flat[0].start()
    flat[1].start()
    for c in range(1, len(chunks)):
        for field in range(4):
            for h in range(halves):
                load(c, field, h).start()

    source = lax.broadcasted_iota(jnp.int32, (cols, cols), 0)
    target = lax.broadcasted_iota(jnp.int32, (cols, cols), 1)
    for i, moved in enumerate((source == target + 1, source == target - 1, (source == target - 1) | (source == target + 2))):
        shift_s[i] = jnp.where(moved, 1.0, 0.0).astype(jnp.bfloat16)

    def halves_of(x):
        whole = x.astype(jnp.bfloat16)
        return whole, (x - whole.astype(jnp.float32)).astype(jnp.bfloat16)

    def moved(parts, i):
        weights = shift_s[i]
        return sum(jnp.dot(p, weights, preferred_element_type=jnp.float32) for p in parts)

    low, high = TILE - 1, TILE + rows
    for h in range(halves):
        span = slice(h * LANES, (h + 1) * LANES)
        for k in range(levels):
            t_s[h, k, low : low + 1, :] = south[k : k + 1, span]
            g_s[h, k, low : low + 1, :] = south[levels + k : levels + k + 1, span]
            u_s[h, k, low : low + 1, :] = south[2 * levels + k : 2 * levels + k + 1, span]
            v_s[h, k, low : low + 1, :] = south[3 * levels + k : 3 * levels + k + 1, span]
            t_s[h, k, high : high + 1, :] = north[NEAR * levels + k : NEAR * levels + k + 1, span]
            t_s[h, k, high + 1 : high + 2, :] = north[FAR * levels + k : FAR * levels + k + 1, span]
            d_s[h, k, high : high + 1, :] = north[DENS * levels + k : DENS * levels + k + 1, span]
            u_s[h, k, high : high + 1, :] = north[ZONAL * levels + k : ZONAL * levels + k + 1, span]
            v_s[h, k, high : high + 1, :] = north[MERID * levels + k : MERID * levels + k + 1, span]
        nf_s[h, rows : rows + 1, :] = north[5 * levels + WET_AT : 5 * levels + WET_AT + 1, span]
    flat[2].wait()
    for h in range(halves):
        nf_s[h, 0:rows, :] = n_s[:, h * LANES : (h + 1) * LANES].astype(jnp.float32)
    for field in range(4):
        for h in range(halves):
            load(0, field, h).wait()

    def make_density(r):
        at = pl.ds(pl.multiple_of(r * TILE + TILE, TILE), TILE)
        for h in range(halves):
            for k in range(levels):
                d_s[h, k, at, :] = density_of(s_s[h, k, at, :], t_s[h, k, at, :])

    lane = lax.broadcasted_iota(jnp.int32, (TILE, LANES), 1)
    is_last = lane == LANES - 1
    is_first = lane == 0
    both = range(halves)

    def to_lane(x, source, target):
        return pltpu.roll(x, (target - source) % LANES, 1)

    def east_of(x, halo, source):
        turned = [pltpu.roll(p, LANES - 1, 1) for p in x] + [to_lane(halo, source, LANES - 1)]
        return [jnp.where(is_last, turned[h + 1], turned[h]) for h in both]

    def west_of(x, halo, source):
        turned = [to_lane(halo, source, 0)] + [pltpu.roll(p, 1, 1) for p in x]
        return [jnp.where(is_first, turned[h], turned[h + 1]) for h in both]

    def mix(r):
        row = pl.multiple_of(r * TILE, TILE)
        at = pl.ds(row + TILE, TILE)
        east = from_east[at, :]
        west = from_west[pl.ds(row, TILE), :]
        order = jnp.bitwise_and(lane, 1) * levels + lax.shift_right_logical(lane, 1)
        pair = jnp.take_along_axis(east, order, axis=1, mode="promise_in_bounds")

        def of(ref):
            x = jnp.concatenate([ref[h, :, at, :] for h in both], axis=-1)
            return halves_of(x.reshape(levels * TILE, cols))

        def keep(ref, y, fix):
            for k in range(levels):
                x = [y[k * TILE : (k + 1) * TILE, h * LANES : (h + 1) * LANES] for h in both]
                fix(k, x)
                for h in both:
                    ref[h, k, at, :] = x[h]

        def fix_far(k, x):
            x[0] = x[0] + jnp.where(is_first, to_lane(west, NEAR * levels + k, 0), 0.0)
            x[-1] = x[-1] + jnp.where(lane >= LANES - 2, to_lane(pair, 2 * k, LANES - 2), 0.0)

        def fix_east(slot):
            def fix(k, x):
                x[-1] = jnp.where(is_last, to_lane(east, slot * levels + k, LANES - 1), x[-1])
            return fix

        def fix_west(slot):
            def fix(k, x):
                x[0] = jnp.where(is_first, to_lane(west, slot * levels + k, 0), x[0])
            return fix

        keep(far_s, moved(of(t_s), 2), fix_far)
        parts = of(u_s)
        keep(ue_s, moved(parts, 0), fix_east(ZONAL))
        keep(uw_s, moved(parts, 1), fix_west(ZONAL))
        parts = of(v_s)
        keep(ve_s, moved(parts, 0), fix_east(MERID))
        keep(vw_s, moved(parts, 1), fix_west(MERID))

    sub16 = lax.broadcasted_iota(jnp.int32, (levels, LANES), 0)
    lane16 = lax.broadcasted_iota(jnp.int32, (levels, LANES), 1)

    def corner(line, slot):
        wide = jnp.broadcast_to(line, (levels, LANES))
        return jnp.sum(jnp.where(lane16 == sub16 + slot * levels, wide, 0.0), axis=1, keepdims=True)

    edge = moved(halves_of(north[ZONAL * levels : (ZONAL + 1) * levels, :]), 1)
    first_lanes = jnp.where(lane16 == 0, corner(from_west[rows : rows + 1, :], ZONAL), edge[:, :LANES])
    for k in range(levels):
        uw_s[0, k, high : high + 1, :] = first_lanes[k : k + 1]
        for h in range(1, halves):
            uw_s[h, k, high : high + 1, :] = edge[k : k + 1, h * LANES : (h + 1) * LANES]
    edge = moved(halves_of(south[3 * levels : 4 * levels, :]), 0)
    last_lanes = jnp.where(lane16 == LANES - 1, corner(from_east[TILE - 1 : TILE, :], MERID), edge[:, -LANES:])
    for k in range(levels):
        ve_s[halves - 1, k, low : low + 1, :] = last_lanes[k : k + 1]
        for h in range(halves - 1):
            ve_s[h, k, low : low + 1, :] = edge[k : k + 1, h * LANES : (h + 1) * LANES]

    make_density(0)
    mix(0)
    flat[0].wait()
    flat[1].wait()

    def tile_step(r, carry):
        for c in range(1, len(chunks)):
            @pl.when(r + 1 == starts[c])
            def _():
                for field in range(4):
                    for h in both:
                        load(c, field, h).wait()

        ahead = jnp.minimum(r + 1, tiles - 1)
        make_density(ahead)
        mix(ahead)

        row = pl.multiple_of(r * TILE, TILE)
        flat_at = pl.ds(row, TILE)

        def rows_of(ref, k, shift):
            return [ref[h, k, pl.ds(row + TILE + shift, TILE), :] for h in both]

        east = from_east[pl.ds(row + 8, TILE), :]
        west = from_west[flat_at, :]
        own = own_west[pl.ds(row + 8, TILE), :]

        def span_of(x):
            up = jnp.where(lane < levels - 1, pltpu.roll(x, LANES - 1, 1), x)
            down = jnp.where(lane > 0, pltpu.roll(x, 1, 1), x)
            return up - down

        t_sum = west + own
        d_near, d_own = to_lane(west, DENS * levels, 0), to_lane(own, DENS * levels, 0)
        t_far = to_lane(west, FAR * levels, 0) + to_lane(own, FAR * levels, 0)
        e1 = jnp.broadcast_to(west[:, E1U_LANE : E1U_LANE + 1], (TILE, LANES))
        e2 = jnp.broadcast_to(west[:, E2U_LANE : E2U_LANE + 1], (TILE, LANES))
        wet_w = jnp.broadcast_to(jnp.minimum(west, own)[:, WET_LANE : WET_LANE + 1], (TILE, LANES))
        d_span = span_of(d_near + d_own)
        tilt = (d_own - d_near) * d_span * span_of(t_sum) * inverse_of(d_span * d_span + 16.0)
        flux_w = diffusivity * e2 / e1 * (own - west - tilt) - e2 / 12.0 * to_lane(west, ZONAL * levels, 0) * (7.0 * t_sum - t_far)
        flux_w = jnp.where(lane.astype(jnp.float32) < wet_w, flux_w, 0.0)

        def flat_of(ref, i):
            return [ref[i, flat_at, h * LANES : (h + 1) * LANES] for h in both]

        e1t, e2t, e1u, e2u, e1v, e2v = (flat_of(e_s, i) for i in range(6))
        fu, fv = flat_of(f_s, 0), flat_of(f_s, 1)
        wet = [nf_s[h, flat_at, :] for h in both]
        wet_n = [nf_s[h, pl.ds(row + 1, TILE), :] for h in both]
        wet_e = east_of(wet, east, WET_LANE)
        u_wet = [jnp.minimum(wet[h], wet_e[h]) for h in both]
        v_wet = [jnp.minimum(wet[h], wet_n[h]) for h in both]
        area = [step_duration / (e1t[h] * e2t[h]) for h in both]
        dt = step_duration

        def speeds(along, across, spin, first_inv, second_inv):
            a, b = first_inv, second_inv
            return (
                0.25 * dt * spin,
                0.125 * dt * across,
                0.5 * dt * along,
                dt * viscosity * a * a,
                dt * viscosity * b * b,
                2.0 * dt * viscosity * (a * a + b * b),
            )

        iu1, iu2 = [1.0 / x for x in e1u], [1.0 / x for x in e2u]
        iv1, iv2 = [1.0 / x for x in e1v], [1.0 / x for x in e2v]
        iso_e = [diffusivity * e2u[h] * iu1[h] for h in both]
        adv_e = [e2u[h] * (1.0 / 12.0) for h in both]
        iso_n = [diffusivity * e1v[h] * iv2[h] for h in both]
        adv_n = [e1v[h] * (1.0 / 12.0) for h in both]
        cu = [speeds(iu1[h], iu2[h], fu[h], iu1[h], iu2[h]) for h in both]
        cv = [speeds(iv2[h], iv1[h], -fv[h], iv1[h], iv2[h]) for h in both]
        pu = [0.5 * gravity * dt * iu1[h] for h in both]
        pv = [0.5 * gravity * dt * iv2[h] for h in both]

        run_e = [jnp.zeros((TILE, LANES), jnp.float32) for _ in both]
        run_n = [jnp.zeros((TILE, LANES), jnp.float32) for _ in both]
        store_at = lambda h: (flat_at, pl.ds(h * LANES, LANES))

        def level_parts(k):
            t, tn, ts, tnn = (rows_of(t_s, k, i) for i in (0, 1, -1, 2))
            d, dn = rows_of(d_s, k, 0), rows_of(d_s, k, 1)
            u, un, us = (rows_of(u_s, k, i) for i in (0, 1, -1))
            v, vn, vs = (rows_of(v_s, k, i) for i in (0, 1, -1))
            te = east_of(t, east, NEAR * levels + k)
            far = rows_of(far_s, k, 0)
            de = east_of(d, east, DENS * levels + k)
            ue, uw, uwn = rows_of(ue_s, k, 0), rows_of(uw_s, k, 0), rows_of(uw_s, k, 1)
            ve, vw, ves = rows_of(ve_s, k, 0), rows_of(vw_s, k, 0), rows_of(ve_s, k, -1)
            out = []
            for h in both:
                se, sn = t[h] + te[h], t[h] + tn[h]
                dde, ddn = de[h] - d[h], dn[h] - d[h]
                he = iso_e[h] * (te[h] - t[h]) - adv_e[h] * u[h] * (7.0 * se - far[h])
                hn = iso_n[h] * (tn[h] - t[h]) - adv_n[h] * v[h] * (7.0 * sn - (ts[h] + tnn[h]))
                out.append((se, d[h] + de[h], he, iso_e[h] * dde, sn, d[h] + dn[h], hn, iso_n[h] * ddn))

                pe, pn = run_e[h] + dde, run_n[h] + ddn
                run_e[h], run_n[h] = pe + dde, pn + ddn
                c1, c2, c3, c4, c5, c6 = cu[h]
                vbar = (v[h] + vs[h]) + (ve[h] + ves[h])
                du = (
                    vbar * (c1 - c2 * (un[h] - us[h]))
                    - u[h] * (c3 * (ue[h] - uw[h]) + c6)
                    + c4 * (ue[h] + uw[h])
                    + c5 * (un[h] + us[h])
                    - pu[h] * pe
                )
                uo_s[(k,) + store_at(h)] = u[h] + jnp.where(u_wet[h] > k, du, 0.0)
                c1, c2, c3, c4, c5, c6 = cv[h]
                ubar = (u[h] + un[h]) + (uw[h] + uwn[h])
                dv = (
                    ubar * (c1 - c2 * (ve[h] - vw[h]))
                    - v[h] * (c3 * (vn[h] - vs[h]) + c6)
                    + c4 * (ve[h] + vw[h])
                    + c5 * (vn[h] + vs[h])
                    - pv[h] * pn
                )
                vo_s[(k,) + store_at(h)] = v[h] + jnp.where(v_wet[h] > k, dv, 0.0)
            return out

        def finish(k, below, here, above):
            fe, fn = [], []
            for h in both:
                t_span, d_span = above[h][0] - below[h][0], above[h][1] - below[h][1]
                flux = here[h][2] - here[h][3] * d_span * t_span * inverse_of(d_span * d_span + 16.0)
                fe.append(jnp.where(u_wet[h] > k, flux, 0.0))
                t_span, d_span = above[h][4] - below[h][4], above[h][5] - below[h][5]
                flux = here[h][6] - here[h][7] * d_span * t_span * inverse_of(d_span * d_span + 16.0)
                fn.append(jnp.where(v_wet[h] > k, flux, 0.0))
            for h in both:
                g_s[h, k, pl.ds(row + TILE, TILE), :] = fn[h]
            fw = west_of(fe, flux_w, k)
            fs = rows_of(g_s, k, -1)
            t = rows_of(t_s, k, 0)
            for h in both:
                change = area[h] * ((fe[h] - fw[h]) + (fn[h] - fs[h]))
                to_s[(k,) + store_at(h)] = t[h] + jnp.where(wet[h] > k, change, 0.0)

        below = here = level_parts(0)
        for k in range(1, levels):
            above = level_parts(k)
            finish(k - 1, below, here, above)
            below, here = here, above
        finish(levels - 1, below, here, here)

        for c in range(len(chunks)):
            @pl.when(r + 1 == starts[c] + chunks[c])
            def _():
                for field in range(3):
                    store(c, field).start()

        return carry

    lax.fori_loop(0, tiles, tile_step, 0)
    for c in range(len(chunks)):
        for field in range(3):
            store(c, field).wait()


def chunk_sizes(tiles):
    sizes = []
    size = 2
    while tiles > 0:
        take = min(size, tiles)
        sizes.append(take)
        tiles -= take
        size += 1
    return tuple(sizes)


def body(
    east_velocity,
    north_velocity,
    heat_anomaly,
    haline_anomaly,
    spacing_lengths,
    planetary_spin,
    ocean_layer_number,
    seam_partner_index,
):
    t, s, u, v = heat_anomaly, haline_anomaly, east_velocity, north_velocity
    levels, rows, cols = t.shape
    lats, lons = lax.axis_size("lat"), lax.axis_size("lon")
    f32 = jnp.float32
    top = rows // TILE - 1
    message = 5 * levels + 8

    low3 = pl.BlockSpec((levels, TILE, cols), lambda i: (0, 0, 0))
    high3 = pl.BlockSpec((levels, TILE, cols), lambda i: (0, top, 0))
    whole = pl.BlockSpec((message, cols), lambda i: (0, 0))
    count = spacing_lengths.shape[0]
    first, second = pl.pallas_call(
        row_pack,
        grid=(1,),
        in_specs=[low3, high3] * 4
        + [
            pl.BlockSpec((count, TILE, cols), lambda i: (0, 0, 0)),
            pl.BlockSpec((count, TILE, cols), lambda i: (0, top, 0)),
            pl.BlockSpec((TILE, cols), lambda i: (0, 0)),
            pl.BlockSpec((TILE, cols), lambda i: (top, 0)),
        ],
        out_specs=[whole, whole],
        out_shape=[jax.ShapeDtypeStruct((message, cols), f32)] * 2,
        name="row_pack",
    )(t, t, s, s, u, u, v, v, spacing_lengths, spacing_lengths, ocean_layer_number, ocean_layer_number)

    axes = ("lon", "lat")

    def place(lat, lon):
        return lon * lats + lat

    swap1, swap2 = [], []
    for lon in range(lons):
        for lat in range(0, lats, 2):
            swap1 += [(place(lat, lon), place(lat + 1, lon)), (place(lat + 1, lon), place(lat, lon))]
        for lat in range(1, lats - 1, 2):
            swap2 += [(place(lat, lon), place(lat + 1, lon)), (place(lat + 1, lon), place(lat, lon))]
        swap2.append((place(lats - 1, lon), place(lats - 1, lons - 1 - lon)))
    got1 = lax.ppermute(first, axes, swap1)
    got2 = lax.ppermute(second, axes, swap2)

    group = 4
    seam = seam_partner_index.reshape(-1, LANES)
    slab = pl.BlockSpec((group, rows, cols), lambda i: (i, 0, 0))
    fixed = lambda *shape: pl.BlockSpec(shape, lambda i: (0,) * len(shape))
    to_east, to_west, north, south = pl.pallas_call(
        lambda *refs: column_pack(group, *refs),
        grid=(levels // group,),
        in_specs=[slab] * 4
        + [fixed(count, rows, cols), fixed(rows, cols)]
        + [fixed(message, cols)] * 4
        + [fixed(*seam.shape)],
        out_specs=[fixed(rows + 8, LANES)] * 2 + [fixed(message, cols), fixed(4 * levels, cols)],
        out_shape=[jax.ShapeDtypeStruct((rows + 8, LANES), f32)] * 2
        + [jax.ShapeDtypeStruct((message, cols), f32), jax.ShapeDtypeStruct((4 * levels, cols), f32)],
        compiler_params=pltpu.CompilerParams(vmem_limit_bytes=60 * 2**20),
        name="column_pack",
    )(t, s, u, v, spacing_lengths, ocean_layer_number, first, second, got1, got2, seam)

    from_west = lax.ppermute(to_east, "lon", [(i, (i + 1) % lons) for i in range(lons)])
    from_east = lax.ppermute(to_west, "lon", [((i + 1) % lons, i) for i in range(lons)])

    chunks = chunk_sizes(rows // TILE)
    halves = cols // LANES
    held = (halves, levels, rows + 2 * TILE, LANES)
    anywhere = pl.BlockSpec(memory_space=pl.ANY)
    near = pl.BlockSpec(memory_space=pltpu.VMEM)
    out = jax.ShapeDtypeStruct((levels, rows, cols), f32)
    return pl.pallas_call(
        lambda *refs: step_kernel(chunks, *refs),
        in_specs=[anywhere] * 7 + [near] * 5,
        out_specs=[anywhere] * 3,
        out_shape=[out] * 3,
        scratch_shapes=[pltpu.VMEM(held, f32)] * 11
        + [
            pltpu.VMEM(spacing_lengths.shape, f32),
            pltpu.VMEM(planetary_spin.shape, f32),
            pltpu.VMEM((rows, cols), jnp.int32),
            pltpu.VMEM((halves, rows + TILE, LANES), f32),
        ]
        + [pltpu.VMEM((levels, rows, cols), f32)] * 3
        + [
            pltpu.VMEM((3, cols, cols), jnp.bfloat16),
            pltpu.SemaphoreType.DMA((len(chunks), 4, halves)),
            pltpu.SemaphoreType.DMA((3,)),
            pltpu.SemaphoreType.DMA((len(chunks), 3)),
        ],
        compiler_params=pltpu.CompilerParams(vmem_limit_bytes=60 * 2**20),
        name="ocean_step",
    )(t, s, u, v, spacing_lengths, planetary_spin, ocean_layer_number, north, south, to_west, from_east, from_west)


def solution(mesh):
    in_specs = (
        P(None, "lat", "lon"),
        P(None, "lat", "lon"),
        P(None, "lat", "lon"),
        P(None, "lat", "lon"),
        P(None, "lat", "lon"),
        P(None, "lat", "lon"),
        P("lat", "lon"),
        P(),
    )
    out_specs = (P(None, "lat", "lon"), P(None, "lat", "lon"), P(None, "lat", "lon"))
    return jax.shard_map(body, mesh=mesh, in_specs=in_specs, out_specs=out_specs, check_vma=False)
```

profile of v0, /device:TPU:13, one launch (start us, length us, event | category | flops | bytes accessed | tf_op | source)
XLA Modules:
  0.0 54.3 jit_solution(7691676146140739257)
XLA Ops:
  0.6 2.1 %row_pack.1 = (f32[88,256]{1,0:T(8,128)}, f32[88,256]{1,0:T(8,128)}) custom-call(f32[16,152,256]{2,1,0:T(8,128)} %refs_0_.3, f32[16,152,256]{2,1,0:T(8,128)} %refs_0_.3, f32[16,152,256]{2,1,0:T(8,128)} %refs_1_.3, f32[16,152,256]{2,1,0:T(8,128)} %refs_1_.3, f32[16,152,256]{2,1,0:T(8,128)} %refs_2_.3, f32[16,152,256]{2,1,0:T(8,128)} %refs_2_.3, ...), custom_call_target="tpu_custom_call" | custom-call | tf_op jit(solution)/shard_map/row_pack/pallas_call | solution.py:510
  2.7 2.0 %collective-permute-start = (f32[88,256]{1,0:T(8,128)}, f32[88,256]{1,0:T(8,128)S(1)}, u32[]{:S(2)}, u32[]{:S(2)}) collective-permute-start(f32[88,256]{1,0:T(8,128)} %get-tuple-element.9.refs_6_), channel_id=1, source_target_pairs={{0,1},{1,0},{2,3},{3,2},{4,5},{5,4},{6,7},{7,6},{8,9},{9,8},{10,11... | collective-permute-start | bytes 270344 | tf_op jit(solution)/shard_map/ppermute | solution.py:537
  4.7 2.8 %collective-permute-start.1 = (f32[88,256]{1,0:T(8,128)}, f32[88,256]{1,0:T(8,128)S(1)}, u32[]{:S(2)}, u32[]{:S(2)}) collective-permute-start(f32[88,256]{1,0:T(8,128)} %get-tuple-element.10.refs_7_), channel_id=1, source_target_pairs={{1,2},{2,1},{3,4},{4,3},{5,6},{6,5},{7,127},{9,10},{10,9},{11,12},... | collective-permute-start | bytes 270344 | tf_op jit(solution)/shard_map/ppermute | solution.py:538
  7.6 0.2 collective-permute-done.refs_8_
  7.8 0.0 copy-start
  7.8 4.8 %collective-permute-done.1.refs_9_ = f32[88,256]{1,0:T(8,128)S(1)} collective-permute-done((f32[88,256]{1,0:T(8,128)}, f32[88,256]{1,0:T(8,128)S(1)}, u32[]{:S(2)}, u32[]{:S(2)}) %collective-permute-start.1) | collective-permute-done | bytes 90144 | tf_op jit(solution)/shard_map/ppermute | solution.py:538
  12.6 0.0 copy-start.1
  12.6 0.0 copy-done
  12.6 0.6 %copy-done.1 = f32[88,256]{1,0:T(8,128)} copy-done((f32[88,256]{1,0:T(8,128)}, f32[88,256]{1,0:T(8,128)S(1)}, u32[]{:S(2)}) %copy-start.1) | copy-done | bytes 90136
  13.3 7.8 %column_pack.1 = (f32[160,128]{1,0:T(8,128)}, f32[160,128]{1,0:T(8,128)}, f32[88,256]{1,0:T(8,128)}, f32[64,256]{1,0:T(8,128)}) custom-call(f32[16,152,256]{2,1,0:T(8,128)} %refs_0_.3, f32[16,152,256]{2,1,0:T(8,128)} %refs_1_.3, f32[16,152,256]{2,1,0:T(8,128)} %refs_2_.3, f32[16,152,256]{2,1,0:T(8,128)} %refs_3_.3, f32[6,152,256]{2,1,0:T(8,128)} %refs_4_.3, ...), custom_call_target="tpu_custom_call" | custom-call | tf_op jit(solution)/shard_map/column_pack/pallas_call | solution.py:544
  21.0 4.5 %collective-permute-start.3 = (f32[160,128]{1,0:T(8,128)}, f32[160,128]{1,0:T(8,128)S(1)}, u32[]{:S(2)}, u32[]{:S(2)}) collective-permute-start(f32[160,128]{1,0:T(8,128)} %get-tuple-element.14), channel_id=1, source_target_pairs={{0,8},{8,16},{16,24},{24,32},{32,40},{40,48},{48,56},{56,64},{64,7... | collective-permute-start | bytes 245768 | tf_op jit(solution)/shard_map/ppermute | solution.py:558
  25.5 0.0 collective-permute-start.2
  25.5 2.2 %collective-permute-done.3.refs_11_ = f32[160,128]{1,0:T(8,128)S(1)} collective-permute-done((f32[160,128]{1,0:T(8,128)}, f32[160,128]{1,0:T(8,128)S(1)}, u32[]{:S(2)}, u32[]{:S(2)}) %collective-permute-start.3) | collective-permute-done | bytes 81952 | tf_op jit(solution)/shard_map/ppermute | solution.py:558
  27.7 0.0 copy-start.2
  27.7 2.8 %collective-permute-done.2.refs_10_ = f32[160,128]{1,0:T(8,128)S(1)} collective-permute-done((f32[160,128]{1,0:T(8,128)}, f32[160,128]{1,0:T(8,128)S(1)}, u32[]{:S(2)}, u32[]{:S(2)}) %collective-permute-start.2) | collective-permute-done | bytes 81952 | tf_op jit(solution)/shard_map/ppermute | solution.py:559
  30.5 0.0 copy-start.3
  30.5 0.0 copy-done.2
  30.5 0.6 %copy-done.3 = f32[160,128]{1,0:T(8,128)} copy-done((f32[160,128]{1,0:T(8,128)}, f32[160,128]{1,0:T(8,128)S(1)}, u32[]{:S(2)}) %copy-start.3) | copy-done | bytes 81944
  31.1 23.2 %ocean_step.1 = (f32[16,152,256]{2,1,0:T(8,128)}, f32[16,152,256]{2,1,0:T(8,128)}, f32[16,152,256]{2,1,0:T(8,128)}) custom-call(f32[16,152,256]{2,1,0:T(8,128)} %refs_0_.3, f32[16,152,256]{2,1,0:T(8,128)} %refs_1_.3, f32[16,152,256]{2,1,0:T(8,128)} %refs_2_.3, f32[16,152,256]{2,1,0:T(8,128)} %refs_3_.3, f32[6,152,256]{2,1,0:T(8,128)} %refs_4_.3, ...), custom_call_target="tpu_custom_call" | custom-call | tf_op jit(solution)/shard_map/ocean_step/pallas_call | solution.py:567
Async XLA Ops:
  2.7 5.1 %collective-permute-start = (f32[88,256]{1,0:T(8,128)}, f32[88,256]{1,0:T(8,128)S(1)}, u32[]{:S(2)}, u32[]{:S(2)}) collective-permute-start(f32[88,256]{1,0:T(8,128)} %get-tuple-element.9.refs_6_), channel_id=1, source_target_pairs={{0,1},{1,0},{2,3},{3,2},{4,5},{5,4},{6,7},{7,6},{8,9},{9,8},{10,11... | collective-permute-start | bytes 270344 | tf_op jit(solution)/shard_map/ppermute | solution.py:537
  4.7 7.9 %collective-permute-start.1 = (f32[88,256]{1,0:T(8,128)}, f32[88,256]{1,0:T(8,128)S(1)}, u32[]{:S(2)}, u32[]{:S(2)}) collective-permute-start(f32[88,256]{1,0:T(8,128)} %get-tuple-element.10.refs_7_), channel_id=1, source_target_pairs={{1,2},{2,1},{3,4},{4,3},{5,6},{6,5},{7,127},{9,10},{10,9},{11,12},... | collective-permute-start | bytes 270344 | tf_op jit(solution)/shard_map/ppermute | solution.py:538
  7.8 4.8 %copy-start = (f32[88,256]{1,0:T(8,128)}, f32[88,256]{1,0:T(8,128)S(1)}, u32[]{:S(2)}) copy-start(f32[88,256]{1,0:T(8,128)S(1)} %collective-permute-done.refs_8_) | copy-start | bytes 270340
  12.6 0.6 %copy-start.1 = (f32[88,256]{1,0:T(8,128)}, f32[88,256]{1,0:T(8,128)S(1)}, u32[]{:S(2)}) copy-start(f32[88,256]{1,0:T(8,128)S(1)} %collective-permute-done.1.refs_9_) | copy-start | bytes 270340
  21.0 6.7 %collective-permute-start.3 = (f32[160,128]{1,0:T(8,128)}, f32[160,128]{1,0:T(8,128)S(1)}, u32[]{:S(2)}, u32[]{:S(2)}) collective-permute-start(f32[160,128]{1,0:T(8,128)} %get-tuple-element.14), channel_id=1, source_target_pairs={{0,8},{8,16},{16,24},{24,32},{32,40},{40,48},{48,56},{56,64},{64,7... | collective-permute-start | bytes 245768 | tf_op jit(solution)/shard_map/ppermute | solution.py:558
  25.5 5.0 %collective-permute-start.2 = (f32[160,128]{1,0:T(8,128)}, f32[160,128]{1,0:T(8,128)S(1)}, u32[]{:S(2)}, u32[]{:S(2)}) collective-permute-start(f32[160,128]{1,0:T(8,128)} %get-tuple-element.13.refs_9_), channel_id=1, source_target_pairs={{8,0},{16,8},{24,16},{32,24},{40,32},{48,40},{56,48},{64,56},{72,6... | collective-permute-start | bytes 245768 | tf_op jit(solution)/shard_map/ppermute | solution.py:559
  27.7 2.8 %copy-start.2 = (f32[160,128]{1,0:T(8,128)}, f32[160,128]{1,0:T(8,128)S(1)}, u32[]{:S(2)}) copy-start(f32[160,128]{1,0:T(8,128)S(1)} %collective-permute-done.3.refs_11_) | copy-start | bytes 245764
  30.5 0.6 %copy-start.3 = (f32[160,128]{1,0:T(8,128)}, f32[160,128]{1,0:T(8,128)S(1)}, u32[]{:S(2)}) copy-start(f32[160,128]{1,0:T(8,128)S(1)} %collective-permute-done.2.refs_10_) | copy-start | bytes 245764
where the time goes:
time: 54.5 us; the launch traced here: 54.3 us
  Pallas kernels  33 us (61%)
  waiting for transfers between devices  10 us (18%)
  starting transfers between devices  9.32 us (17%)
  local copies, waits for them, and re-layouts  1.27 us (2%)
  between operations  0.65 us (1%)
    pallas_call x1, Pallas kernels, body(): pl.pallas_call(lambda *refs: step_kernel(chunks, *refs), in_specs=[anywhe...  23.2 us
    pallas_call x1, Pallas kernels, body(): pl.pallas_call(lambda *refs: column_pack(group, *refs), grid=(levels // g...  7.75 us
    ppermute x1, waiting for transfers between devices, body(): got2 = lax.ppermute(second, axes, swap2)  4.79 us
    ppermute x1, starting transfers between devices, body(): lax.ppermute(to_east, 'lon', [(i, (i + 1) % lons) for i in range(lons)])  4.48 us
    ppermute x1, starting transfers between devices, body(): got2 = lax.ppermute(second, axes, swap2)  2.82 us
    ppermute x1, waiting for transfers between devices, body(): lax.ppermute(to_west, 'lon', [((i + 1) % lons, i) for i in range(lons)])  2.78 us
    ppermute x1, waiting for transfers between devices, body(): lax.ppermute(to_east, 'lon', [(i, (i + 1) % lons) for i in range(lons)])  2.19 us
    pallas_call x1, Pallas kernels, body(): pl.pallas_call(row_pack, grid=(1,), in_specs=[low3, high3] * 4 + [pl.Bloc...  2.1 us
  transfers between devices with their start and end apart: 4, of which 4 were waited for; matrix products, arithmetic and copies ran while one was open for 0% of the time, Pallas kernels for 0%

commit v1 on v0

v1 whole, which is shorter than its diff:
```python
import jax
import jax.numpy as jnp
from jax import lax
from jax.experimental import pallas as pl
from jax.experimental.pallas import tpu as pltpu
from jax.sharding import PartitionSpec as P

LANES = 128
TILE = 8

step_duration = 0.25
viscosity = 0.05
diffusivity = 0.3
expansion_coefficient = 0.6
haline_contraction = 0.8
gravity = 0.1

NEAR, FAR, SALT, ZONAL, MERID = 0, 1, 2, 3, 4
E1V_AT, E2V_AT, WET_AT = 0, 1, 2
HEAT_LANE, SALT_LANE, ZONAL_LANE, MERID_LANE = 0, 40, 56, 72
E1U_LANE, E2U_LANE, WET_LANE = 96, 97, 98


def density_of(salinity, heat):
    return haline_contraction * salinity - expansion_coefficient * heat


def inverse_of(x):
    return pltpu.reciprocal(x, approx=True)


def row_pack(t_lo, t_hi, s_lo, s_hi, u_lo, u_hi, v_lo, v_hi, e_lo, e_hi, n_lo, n_hi, first, second):
    levels = t_lo.shape[0]
    even = lax.rem(lax.axis_index("lat"), 2) == 0

    def put(slot, high, low):
        rows = pl.ds(slot * levels, levels)
        first[rows] = jnp.where(even, high, low)
        second[rows] = jnp.where(even, low, high)

    near_hi, near_lo = t_hi[:, 7, :], t_lo[:, 0, :]
    put(NEAR, near_hi, near_lo)
    put(FAR, t_hi[:, 6, :], t_lo[:, 1, :])
    put(SALT, s_hi[:, 7, :], s_lo[:, 0, :])
    put(ZONAL, u_hi[:, 7, :], u_lo[:, 0, :])
    put(MERID, v_hi[:, 7, :], v_lo[:, 0, :])
    base = 5 * levels
    high = jnp.concatenate([e_hi[4, 7:8], e_hi[5, 7:8], n_hi[7:8].astype(jnp.float32), jnp.zeros((5, e_hi.shape[2]), jnp.float32)], axis=0)
    low = jnp.concatenate([e_lo[4, 0:1], e_lo[5, 0:1], n_lo[0:1].astype(jnp.float32), jnp.zeros((5, e_lo.shape[2]), jnp.float32)], axis=0)
    first[base : base + 8] = jnp.where(even, high, low)
    second[base : base + 8] = jnp.where(even, low, high)


def vertical_span(x):
    return jnp.concatenate([x[1:], x[-1:]], axis=0) - jnp.concatenate([x[:1], x[:-1]], axis=0)


def corners(u1, u2, v1, v2, seam, east_in, west_in, east_out, west_out):
    levels, cols = u1.shape
    lat, lon = lax.axis_index("lat"), lax.axis_index("lon")
    lats, lons = lax.axis_size("lat"), lax.axis_size("lon")
    even = lax.rem(lat, 2) == 0
    is_top = lat == lats - 1
    per = cols // LANES
    pick = seam[pl.ds(lon * per + per - 1, 1), LANES - 1 : LANES] - (lons - 1 - lon) * cols
    pick = jnp.where(is_top, pick, cols - 1)
    u = jnp.where(even, u1[...], u2[...])
    u = jnp.where(is_top, -u, u)
    here = lax.broadcasted_iota(jnp.int32, (levels, cols), 1) == pick
    u = jnp.sum(jnp.where(here, u, 0.0), axis=1, keepdims=True)
    v = jnp.where(lat == 0, 0.0, jnp.where(even, v2[:, 0:1], v1[:, 0:1]))
    sub16 = lax.broadcasted_iota(jnp.int32, (levels, LANES), 0)
    lane16 = lax.broadcasted_iota(jnp.int32, (levels, LANES), 1)

    def line(x, base):
        return jnp.sum(jnp.where(lane16 == sub16 + base, x, 0.0), axis=0, keepdims=True)

    east_out[...] = jnp.broadcast_to(line(u, ZONAL_LANE), (8, LANES))
    west_out[...] = jnp.broadcast_to(line(v, MERID_LANE + 1), (8, LANES))


def halo_rows(mine1, mine2, got1, got2, seam, north_out, south_out):
    levels = (mine1.shape[0] - 8) // 5
    cols = mine1.shape[1]
    lat, lon = lax.axis_index("lat"), lax.axis_index("lon")
    lats, lons = lax.axis_size("lat"), lax.axis_size("lon")
    even = lax.rem(lat, 2) == 0
    is_top = lat == lats - 1
    is_bottom = lat == 0
    north_rows = got1.shape[0]
    for h in range(cols // LANES):
        span = slice(h * LANES, (h + 1) * LANES)
        pick = seam[pl.ds(lon * (cols // LANES) + h, 1), :] - (lons - 1 - lon) * cols
        pick = jnp.where(is_top, pick, lax.broadcasted_iota(jnp.int32, (1, LANES), 1) + h * LANES)
        pick = jnp.broadcast_to(pick, (TILE, LANES))
        inner = jnp.bitwise_and(pick, LANES - 1)
        for row in range(0, north_rows, TILE):
            total = None
            for g in range(cols // LANES):
                piece = slice(g * LANES, (g + 1) * LANES)
                source = jnp.where(even, got1[row : row + TILE, piece], got2[row : row + TILE, piece])
                taken = jnp.take_along_axis(source, inner, axis=1, mode="promise_in_bounds")
                taken = jnp.where(pick >= g * LANES, taken, 0.0) if g == 0 else taken
                total = taken if total is None else jnp.where(pick >= g * LANES, taken, total)
            if ZONAL * levels <= row < (MERID + 1) * levels:
                total = jnp.where(is_top, -total, total)
            north_out[row : row + TILE, span] = total
    def south(slot):
        part = slice(slot * levels, (slot + 1) * levels)
        return jnp.where(is_bottom, 0.0, jnp.where(even, got2[part], got1[part]))

    def own(slot):
        part = slice(slot * levels, (slot + 1) * levels)
        return jnp.where(even, mine2[part], mine1[part])

    tail = slice(5 * levels, 5 * levels + 8)
    coef = jnp.where(even, got2[tail], got1[tail])
    own_wet = jnp.where(even, mine2[tail], mine1[tail])[WET_AT : WET_AT + 1]
    e1v = jnp.where(is_bottom, 1.0, coef[E1V_AT : E1V_AT + 1])
    e2v = jnp.where(is_bottom, 1.0, coef[E2V_AT : E2V_AT + 1])
    wet = jnp.where(is_bottom, 0.0, coef[WET_AT : WET_AT + 1])
    t_near, t_far, v_near = south(NEAR), south(FAR), south(MERID)
    t_own, t_next = own(NEAR), own(FAR)
    d_near, d_own = density_of(south(SALT), t_near), density_of(own(SALT), t_own)
    t_sum = t_near + t_own
    adv = (e1v / 12.0) * v_near * (7.0 * t_sum - (t_far + t_next))
    d_span = vertical_span(d_near + d_own)
    tilt = (d_own - d_near) * d_span * vertical_span(t_sum) / (d_span * d_span + 16.0)
    iso = (diffusivity * e1v / e2v) * (t_own - t_near - tilt)
    level = lax.broadcasted_iota(jnp.int32, (levels, cols), 0).astype(jnp.float32)
    flux = jnp.where(level < jnp.minimum(wet, own_wet), iso - adv, 0.0)
    south_out[0:levels] = t_near
    south_out[levels : 2 * levels] = flux
    south_out[2 * levels : 3 * levels] = south(ZONAL)
    south_out[3 * levels : 4 * levels] = v_near


def column_pack(group, t, s, u, v, e, n, east_out, west_out):
    rows, cols = t.shape[1:]
    step = pl.program_id(0)
    lane = lax.broadcasted_iota(jnp.int32, (rows, LANES), 1)
    pair = lax.shift_right_logical(lane, 1)
    first = slice(0, LANES)
    last = slice(cols - LANES, cols)

    @pl.when(step == 0)
    def _():
        n_f = n[...].astype(jnp.float32)
        hi = jnp.where(lane == E1U_LANE, pltpu.roll(e[0, :, last], (E1U_LANE + 1) % LANES, 1), 0.0)
        hi = jnp.where(lane == E2U_LANE, pltpu.roll(e[1, :, last], (E2U_LANE + 1) % LANES, 1), hi)
        east_out[0:rows] = jnp.where(lane == WET_LANE, pltpu.roll(n_f[:, last], (WET_LANE + 1) % LANES, 1), hi)
        west_out[8 : rows + 8] = jnp.where(lane == WET_LANE, pltpu.roll(n_f[:, first], WET_LANE, 1), 0.0)
        east_out[rows : rows + 8] = jnp.zeros((8, LANES), jnp.float32)
        west_out[0:8] = jnp.zeros((8, LANES), jnp.float32)

    hi = east_out[0:rows]
    lo = west_out[8 : rows + 8]
    for kk in range(group):
        k = step * group + kk
        for field, base in ((t, HEAT_LANE), (s, SALT_LANE), (u, ZONAL_LANE), (v, MERID_LANE)):
            ends = jnp.where(lane < LANES // 2, field[kk, :, first], field[kk, :, last])
            if field is t:
                ends = pltpu.roll(ends, 2 * k + 2, 1)
                hi = jnp.where(pair == k, ends, hi)
                lo = jnp.where(pair == k + 1, ends, lo)
            else:
                ends = pltpu.roll(ends, base + 1 + k, 1)
                hi = jnp.where(lane == base + k, ends, hi)
                lo = jnp.where(lane == base + 1 + k, ends, lo)
    east_out[0:rows] = hi
    west_out[8 : rows + 8] = lo


def step_kernel(
    t_hbm, s_hbm, u_hbm, v_hbm, e_hbm, f_hbm, n_hbm, north_hbm, south_hbm, own_hbm, from_east_hbm, from_west_hbm,
    u_out, v_out, t_out,
    north, south, own_west, from_east, from_west, t_s, s_s, u_s, v_s, d_s, g_s, mixed_a, uw_a, ve_a, mixed_b, uw_b, ve_b, e_s, f_s, n_s, nf_s, uo_s, vo_s, to_s, move_s, rim_s, mask_s,
    in_sem, flat_sem, out_sem,
):
    levels, rows, cols = t_hbm.shape
    tiles = rows // TILE
    halves = cols // LANES
    both = range(halves)
    pairs = (tiles - 1) // 2
    assert tiles == 2 * pairs + 1

    fields = ((t_hbm, t_s), (s_hbm, s_s), (u_hbm, u_s), (v_hbm, v_s))

    def load(first, count, unit):
        span = pl.ds(first * TILE, count * TILE)
        held = pl.ds(first * TILE + TILE, count * TILE)
        for hbm, vmem in fields:
            for h in both:
                pltpu.make_async_copy(
                    hbm.at[:, span, pl.ds(h * LANES, LANES)], vmem.at[h, :, held, :], in_sem.at[unit]
                ).start()

    def loaded(count, unit):
        span = pl.ds(0, len(fields) * halves * count * TILE)
        pltpu.make_async_copy(t_hbm.at[:, span, pl.ds(0, LANES)], t_s.at[0, :, span, :], in_sem.at[unit]).wait()

    outs = ((uo_s, u_out), (vo_s, v_out), (to_s, t_out))

    def store(row, count):
        span = pl.ds(row, count * TILE)
        for i, (vmem, hbm) in enumerate(outs):
            pltpu.make_async_copy(vmem.at[:, span, :], hbm.at[:, span, :], out_sem.at[i]).start()

    flat = [
        pltpu.make_async_copy(hbm, vmem, flat_sem.at[i])
        for i, (hbm, vmem) in enumerate(
            (
                (e_hbm, e_s),
                (f_hbm, f_s),
                (n_hbm, n_s),
                (north_hbm, north),
                (south_hbm, south),
                (own_hbm, own_west),
                (from_east_hbm, from_east),
                (from_west_hbm, from_west),
            )
        )
    ]
    for copy in flat[2:]:
        copy.start()
    load(0, 1, 0)
    load(1, 2, 1)
    flat[0].start()
    flat[1].start()
    for unit in range(2, pairs + 1):
        load(2 * unit - 1, 2, unit)

    source = lax.broadcasted_iota(jnp.int32, (cols, cols), 0)
    target = lax.broadcasted_iota(jnp.int32, (cols, cols), 1)
    apart = source - target

    def matrix(*terms):
        total = jnp.zeros((cols, cols), jnp.float32)
        for where, value in terms:
            total = jnp.where(where, value, total)
        return total.astype(jnp.bfloat16)

    at = [apart == i for i in range(-1, 3)]
    move_s[0] = matrix((at[0], -1.0), (at[1], 7.0), (at[2], 7.0), (at[3], -1.0))
    move_s[1] = matrix((at[0], 1.0))
    move_s[2] = matrix((at[2], 1.0))
    origin = jnp.bitwise_and(source, LANES - 1)
    odd = jnp.bitwise_and(origin, 1) == 1
    west_end, east_end = target == 0, target == cols - 1
    heat_east, heat_west = origin < 32, (origin >= 32) & (origin < 64) & odd
    rim_s[0] = matrix(
        (heat_east & ~odd & (target == cols - 2), -1.0),
        (heat_east & ~odd & east_end, 7.0),
        (heat_east & odd & east_end, -1.0),
        (heat_west & west_end, -1.0),
    )
    western = jnp.bitwise_and(origin, 16) == 16
    rim_s[1] = matrix(((origin >= 64) & western & west_end, 1.0))
    rim_s[2] = matrix(
        ((origin >= 64) & ~western & east_end, 1.0),
        (heat_east & ~odd & east_end, 1.0),
        ((origin >= 32) & (origin < 64) & ~odd & east_end, 1.0),
    )

    for copy in flat[2:]:
        copy.wait()
    low, high = TILE - 1, TILE + rows
    north_density = density_of(
        north[SALT * levels : (SALT + 1) * levels, :], north[NEAR * levels : (NEAR + 1) * levels, :]
    )
    for h in both:
        span = slice(h * LANES, (h + 1) * LANES)
        for k in range(levels):
            t_s[h, k, low : low + 1, :] = south[k : k + 1, span]
            g_s[h, k, low : low + 1, :] = south[levels + k : levels + k + 1, span]
            u_s[h, k, low : low + 1, :] = south[2 * levels + k : 2 * levels + k + 1, span]
            v_s[h, k, low : low + 1, :] = south[3 * levels + k : 3 * levels + k + 1, span]
            t_s[h, k, high : high + 1, :] = north[NEAR * levels + k : NEAR * levels + k + 1, span]
            t_s[h, k, high + 1 : high + 2, :] = north[FAR * levels + k : FAR * levels + k + 1, span]
            d_s[h, k, high : high + 1, :] = north_density[k : k + 1, span]
            u_s[h, k, high : high + 1, :] = north[ZONAL * levels + k : ZONAL * levels + k + 1, span]
            v_s[h, k, high : high + 1, :] = north[MERID * levels + k : MERID * levels + k + 1, span]
        nf_s[h, rows : rows + 1, :] = north[5 * levels + WET_AT : 5 * levels + WET_AT + 1, span]
    for h in both:
        nf_s[h, 0:rows, :] = n_s[:, h * LANES : (h + 1) * LANES].astype(jnp.float32)
    loaded(1, 0)
    loaded(2, 1)

    lane = lax.broadcasted_iota(jnp.int32, (TILE, LANES), 1)
    is_last = lane == LANES - 1
    is_first = lane == 0
    from_rim_west = ((lane >= 32) & (lane < 64)) | ((lane >= 80) & (lane < 96)) | (lane >= 112)
    rim_source = jnp.where(
        lane < 32,
        lane + 2,
        jnp.where(
            lane < 64,
            lane - 32,
            jnp.where(
                lane < 80,
                lane - 64 + ZONAL_LANE + 1,
                jnp.where(
                    lane < 96,
                    lane - 80 + ZONAL_LANE,
                    jnp.where(lane < 112, lane - 96 + MERID_LANE + 1, lane - 112 + MERID_LANE),
                ),
            ),
        ),
    )
    lane2 = lax.broadcasted_iota(jnp.int32, (2 * TILE, LANES), 1)
    second = lax.broadcasted_iota(jnp.int32, (2 * TILE, LANES), 0) >= TILE
    level2 = jnp.where(lane2 < 64, lax.shift_right_logical(jnp.bitwise_and(lane2, 31), 1), jnp.bitwise_and(lane2, 15))
    level2 = level2 - jnp.where(second, 1, 0)
    for_density = (lane2 >= 32) & (lane2 < 64) & (jnp.bitwise_and(lane2, 1) == 0)
    kinds = ((lane2 < 64) & ~for_density, (lane2 >= 64) & (lane2 < 96), lane2 >= 96, for_density)
    for i, kind in enumerate(kinds):
        for p in range(levels // 2):
            mask_s[i, p] = jnp.where(kind & (level2 == 2 * p), 1.0, 0.0).astype(jnp.bfloat16)
    density_lane = (lane >= 32) & (lane < 64) & (jnp.bitwise_and(lane, 1) == 0)
    salt_source = jnp.bitwise_and(SALT_LANE + 1 + lax.shift_right_logical(lane - 32, 1), LANES - 1)
    heat_source = jnp.bitwise_and(lane - 30, LANES - 1)

    def to_lane(x, source, target):
        return pltpu.roll(x, (target - source) % LANES, 1)

    def east_of(x, halo, source):
        turned = [pltpu.roll(p, LANES - 1, 1) for p in x] + [to_lane(halo, source, LANES - 1)]
        return [jnp.where(is_last, turned[h + 1], turned[h]) for h in both]

    def west_of(x, halo, source):
        turned = [to_lane(halo, source, 0)] + [pltpu.roll(p, 1, 1) for p in x]
        return [jnp.where(is_first, turned[h], turned[h + 1]) for h in both]

    def two_parts(x):
        high_part = x.astype(jnp.bfloat16)
        return [high_part, (x - high_part.astype(jnp.float32)).astype(jnp.bfloat16)]

    def moved(parts, edges, i):
        y = jnp.dot(edges, rim_s[i], preferred_element_type=jnp.float32) if edges is not None else 0.0
        for p in parts:
            y = y + jnp.dot(p, move_s[i], preferred_element_type=jnp.float32)
        return y

    def mix(r, kept, previous):
        mixed, uw_s, ve_s = kept
        row = pl.multiple_of(r * TILE, TILE)

        def turned(x, order):
            return jnp.take_along_axis(x, order, axis=1, mode="promise_in_bounds")

        east = from_east[pl.ds(row + TILE, TILE), :]
        x = jnp.where(from_rim_west, turned(from_west[pl.ds(row, TILE), :], rim_source), turned(east, rim_source))
        x = jnp.where(density_lane, density_of(turned(east, salt_source), turned(east, heat_source)), x)
        twice = [jnp.concatenate([p, p], axis=0) for p in two_parts(x)]

        def spread(kind):
            split = [[p * mask_s[kind, i] for i in range(levels // 2)] for p in twice]
            return jnp.concatenate([jnp.concatenate(q, axis=0) for q in split], axis=1)

        rim_t, rim_u, rim_v, rim_d = (spread(kind) for kind in range(4))

        def of(values):
            return two_parts(jnp.concatenate(values, axis=-1).reshape(levels * TILE, cols))

        def held_in(ref):
            return [ref[h, :, pl.ds(row + TILE, TILE), :] for h in both]

        def piece(y, i, h):
            count = levels * TILE
            return y[i * count : (i + 1) * count, h * LANES : (h + 1) * LANES].reshape(levels, TILE, LANES)

        d = [density_of(salt, heat) for salt, heat in zip(held_in(s_s), held_in(t_s))]
        for h in both:
            d_s[h, :, pl.ds(row + TILE, TILE), :] = d[h]
        parts = [of(held_in(u_s)), of(held_in(v_s)), of(held_in(t_s)), of(d)]
        y = moved([jnp.concatenate(p, axis=0) for p in zip(*parts)], jnp.concatenate([rim_u, rim_v, rim_t, rim_d], axis=0), 2)
        for h in both:
            mixed[0, h] = piece(y, 0, h)
            ve_s[h, :, TILE : 2 * TILE, :] = piece(y, 1, h)
            mixed[3, h] = piece(y, 2, h)
            mixed[4, h] = piece(y, 3, h)
        y = moved(parts[2], rim_t, 0)
        for h in both:
            mixed[2, h] = piece(y, 0, h)
        y = moved([jnp.concatenate(p, axis=0) for p in zip(*parts[:2])], jnp.concatenate([rim_u, rim_v], axis=0), 1)
        for h in both:
            uw = piece(y, 0, h)
            uw_s[h, :, 0:TILE, :] = uw
            previous[1][h, :, TILE : TILE + 1, :] = uw[:, 0:1, :]
            mixed[1, h] = piece(y, 1, h)

    sub16 = lax.broadcasted_iota(jnp.int32, (levels, LANES), 0)
    lane16 = lax.broadcasted_iota(jnp.int32, (levels, LANES), 1)

    def corner(line, base):
        wide = jnp.broadcast_to(line, (levels, LANES))
        return jnp.sum(jnp.where(lane16 == sub16 + base, wide, 0.0), axis=1, keepdims=True)

    edge = moved(two_parts(south[3 * levels : 4 * levels, :]), None, 2)
    edge = [edge[:, h * LANES : (h + 1) * LANES] for h in both]
    edge[-1] = jnp.where(lane16 == LANES - 1, corner(from_east[TILE - 1 : TILE, :], MERID_LANE + 1), edge[-1])
    for h in both:
        for k in range(levels):
            ve_a[h, k, TILE - 1 : TILE, :] = edge[h][k : k + 1]

    def advance(r, kept, following):
        mixed, uw_s, ve_s = kept
        for h in both:
            following[2][h, :, TILE - 1 : TILE, :] = ve_s[h, :, 2 * TILE - 1 : 2 * TILE, :]
        row = pl.multiple_of(r * TILE, TILE)
        flat_at = pl.ds(row, TILE)

        def rows_of(ref, k, shift):
            return [ref[h, k, pl.ds(row + TILE + shift, TILE), :] for h in both]

        east = from_east[pl.ds(row + TILE, TILE), :]
        west = from_west[flat_at, :]
        own = own_west[pl.ds(row + TILE, TILE), :]

        def span_of(x):
            up = jnp.where(lane < levels - 1, pltpu.roll(x, LANES - 1, 1), x)
            down = jnp.where(lane > 0, pltpu.roll(x, 1, 1), x)
            return up - down

        def heat_lane(x, offset):
            order = jnp.bitwise_and(2 * lane + offset, LANES - 1)
            return jnp.take_along_axis(x, order, axis=1, mode="promise_in_bounds")

        t_near, t_own = heat_lane(west, 1), heat_lane(own, 2)
        t_sum, t_far = t_near + t_own, heat_lane(west, 0) + heat_lane(own, 3)
        d_near = density_of(to_lane(west, SALT_LANE, 0), t_near)
        d_own = density_of(to_lane(own, SALT_LANE + 1, 0), t_own)
        e1 = jnp.broadcast_to(west[:, E1U_LANE : E1U_LANE + 1], (TILE, LANES))
        e2 = jnp.broadcast_to(west[:, E2U_LANE : E2U_LANE + 1], (TILE, LANES))
        wet_w = jnp.broadcast_to(jnp.minimum(west, own)[:, WET_LANE : WET_LANE + 1], (TILE, LANES))
        d_span = span_of(d_near + d_own)
        tilt = (d_own - d_near) * d_span * span_of(t_sum) * inverse_of(d_span * d_span + 16.0)
        flux_w = diffusivity * e2 * inverse_of(e1) * (t_own - t_near - tilt)
        flux_w = flux_w - e2 * (1.0 / 12.0) * to_lane(west, ZONAL_LANE, 0) * (7.0 * t_sum - t_far)
        flux_w = jnp.where(lane.astype(jnp.float32) < wet_w, flux_w, 0.0)

        def flat_of(ref, i):
            return [ref[i, flat_at, h * LANES : (h + 1) * LANES] for h in both]

        e1t, e2t, e1u, e2u, e1v, e2v = (flat_of(e_s, i) for i in range(6))
        fu, fv = flat_of(f_s, 0), flat_of(f_s, 1)
        wet = [nf_s[h, flat_at, :] for h in both]
        wet_n = [nf_s[h, pl.ds(row + 1, TILE), :] for h in both]
        wet_e = east_of(wet, east, WET_LANE)
        u_wet = [jnp.minimum(wet[h], wet_e[h]) for h in both]
        v_wet = [jnp.minimum(wet[h], wet_n[h]) for h in both]
        dt = step_duration
        area = [dt * inverse_of(e1t[h] * e2t[h]) for h in both]

        def speeds(spin, along, across, a, b):
            c4, c5 = dt * viscosity * a * a, dt * viscosity * b * b
            return 0.25 * dt * spin, 0.125 * dt * across, 0.5 * dt * along, c4, c5, 2.0 * (c4 + c5)

        iu1, iu2 = [inverse_of(x) for x in e1u], [inverse_of(x) for x in e2u]
        iv1, iv2 = [inverse_of(x) for x in e1v], [inverse_of(x) for x in e2v]
        iso_e = [diffusivity * e2u[h] * iu1[h] for h in both]
        adv_e = [e2u[h] * (1.0 / 12.0) for h in both]
        iso_n = [diffusivity * e1v[h] * iv2[h] for h in both]
        adv_n = [e1v[h] * (1.0 / 12.0) for h in both]
        cu = [speeds(fu[h], iu1[h], iu2[h], iu1[h], iu2[h]) for h in both]
        cv = [speeds(-fv[h], iv2[h], iv1[h], iv1[h], iv2[h]) for h in both]
        pu = [0.5 * gravity * dt * iu1[h] for h in both]
        pv = [0.5 * gravity * dt * iv2[h] for h in both]

        store_at = lambda h: (flat_at, pl.ds(h * LANES, LANES))
        zero = jnp.zeros((TILE, LANES), jnp.float32)

        run = [zero for _ in both]

        def east_parts(k):
            t, d, u = rows_of(t_s, k, 0), rows_of(d_s, k, 0), rows_of(u_s, k, 0)
            un, us = rows_of(u_s, k, 1), rows_of(u_s, k, -1)
            ue, wide, te, de = ([mixed[i, h, k] for h in both] for i in (0, 2, 3, 4))
            uw = [uw_s[h, k, 0:TILE, :] for h in both]
            v, vs = rows_of(v_s, k, 0), rows_of(v_s, k, -1)
            vbar = [
                (v[h] + vs[h]) + (ve_s[h, k, TILE : 2 * TILE, :] + ve_s[h, k, TILE - 1 : 2 * TILE - 1, :]) for h in both
            ]
            out = []
            for h in both:
                rise = de[h] - d[h]
                direct = iso_e[h] * (te[h] - t[h]) - adv_e[h] * u[h] * wide[h]
                out.append((t[h] + te[h], d[h] + de[h], direct, iso_e[h] * rise))
                press = run[h] + rise
                run[h] = press + rise
                c1, c2, c3, c4, c5, c6 = cu[h]
                du = (
                    vbar[h] * (c1 - c2 * (un[h] - us[h]))
                    - u[h] * (c3 * (ue[h] - uw[h]) + c6)
                    + c4 * (ue[h] + uw[h])
                    + c5 * (un[h] + us[h])
                    - pu[h] * press
                )
                uo_s[(k,) + store_at(h)] = u[h] + jnp.where(u_wet[h] > k, du, 0.0)
            return out

        def flux_of(below, here, above, open_face):
            t_span, d_span = above[0] - below[0], above[1] - below[1]
            flux = here[2] - here[3] * d_span * t_span * inverse_of(d_span * d_span + 16.0)
            return jnp.where(open_face, flux, 0.0)

        def east_finish(k, below, here, above):
            fe = [flux_of(below[h], here[h], above[h], u_wet[h] > k) for h in both]
            fw = west_of(fe, flux_w, k)
            for h in both:
                to_s[(k,) + store_at(h)] = fe[h] - fw[h]

        below = here = east_parts(0)
        for k in range(1, levels):
            above = east_parts(k)
            east_finish(k - 1, below, here, above)
            below, here = here, above
        east_finish(levels - 1, below, here, here)

        run = [zero for _ in both]

        def north_parts(k):
            t, tn, ts, tnn = (rows_of(t_s, k, i) for i in (0, 1, -1, 2))
            d, dn = rows_of(d_s, k, 0), rows_of(d_s, k, 1)
            v, vn, vs = (rows_of(v_s, k, i) for i in (0, 1, -1))
            ve, vw = [ve_s[h, k, TILE : 2 * TILE, :] for h in both], [mixed[1, h, k] for h in both]
            u, un = rows_of(u_s, k, 0), rows_of(u_s, k, 1)
            ubar = [(u[h] + un[h]) + (uw_s[h, k, 0:TILE, :] + uw_s[h, k, 1 : TILE + 1, :]) for h in both]
            out = []
            for h in both:
                rise, pair = dn[h] - d[h], t[h] + tn[h]
                direct = iso_n[h] * (tn[h] - t[h]) - adv_n[h] * v[h] * (7.0 * pair - (ts[h] + tnn[h]))
                out.append((pair, d[h] + dn[h], direct, iso_n[h] * rise))
                press = run[h] + rise
                run[h] = press + rise
                c1, c2, c3, c4, c5, c6 = cv[h]
                dv = (
                    ubar[h] * (c1 - c2 * (ve[h] - vw[h]))
                    - v[h] * (c3 * (vn[h] - vs[h]) + c6)
                    + c4 * (ve[h] + vw[h])
                    + c5 * (vn[h] + vs[h])
                    - pv[h] * press
                )
                vo_s[(k,) + store_at(h)] = v[h] + jnp.where(v_wet[h] > k, dv, 0.0)
            return out

        def north_finish(k, below, here, above):
            for h in both:
                fn = flux_of(below[h], here[h], above[h], v_wet[h] > k)
                g_s[h, k, pl.ds(row + TILE, TILE), :] = fn
                fs = g_s[h, k, pl.ds(row + TILE - 1, TILE), :]
                at_h = (k,) + store_at(h)
                change = area[h] * (to_s[at_h] + (fn - fs))
                to_s[at_h] = t_s[h, k, pl.ds(row + TILE, TILE), :] + jnp.where(wet[h] > k, change, 0.0)

        below = here = north_parts(0)
        for k in range(1, levels):
            above = north_parts(k)
            north_finish(k - 1, below, here, above)
            below, here = here, above
        north_finish(levels - 1, below, here, here)

    set_a, set_b = (mixed_a, uw_a, ve_a), (mixed_b, uw_b, ve_b)
    mix(0, set_a, set_b)
    flat[0].wait()
    flat[1].wait()

    def two_tiles(i, carry):
        @pl.when(i + 2 <= pairs)
        def _():
            loaded(2, i + 2)

        mix(2 * i + 1, set_b, set_a)
        advance(2 * i, set_a, set_b)
        mix(2 * i + 2, set_a, set_b)
        advance(2 * i + 1, set_b, set_a)
        store(pl.multiple_of(i * 2 * TILE, 2 * TILE), 2)
        return carry

    lax.fori_loop(0, pairs, two_tiles, 0)
    edge = moved(two_parts(north[ZONAL * levels : (ZONAL + 1) * levels, :]), None, 1)
    edge = [edge[:, h * LANES : (h + 1) * LANES] for h in both]
    edge[0] = jnp.where(lane16 == 0, corner(from_west[rows : rows + 1, :], ZONAL_LANE), edge[0])
    for h in both:
        for k in range(levels):
            uw_a[h, k, TILE : TILE + 1, :] = edge[h][k : k + 1]
    advance(jnp.int32(2 * pairs), set_a, set_b)
    store(2 * pairs * TILE, 1)
    for i, (vmem, hbm) in enumerate(outs):
        pltpu.make_async_copy(vmem, hbm, out_sem.at[i]).wait()


def body(
    east_velocity,
    north_velocity,
    heat_anomaly,
    haline_anomaly,
    spacing_lengths,
    planetary_spin,
    ocean_layer_number,
    seam_partner_index,
):
    t, s, u, v = heat_anomaly, haline_anomaly, east_velocity, north_velocity
    levels, rows, cols = t.shape
    lats, lons = lax.axis_size("lat"), lax.axis_size("lon")
    f32 = jnp.float32
    top = rows // TILE - 1
    message = 5 * levels + 8

    low3 = pl.BlockSpec((levels, TILE, cols), lambda i: (0, 0, 0))
    high3 = pl.BlockSpec((levels, TILE, cols), lambda i: (0, top, 0))
    whole = pl.BlockSpec((message, cols), lambda i: (0, 0))
    count = spacing_lengths.shape[0]
    first, second = pl.pallas_call(
        row_pack,
        grid=(1,),
        in_specs=[low3, high3] * 4
        + [
            pl.BlockSpec((count, TILE, cols), lambda i: (0, 0, 0)),
            pl.BlockSpec((count, TILE, cols), lambda i: (0, top, 0)),
            pl.BlockSpec((TILE, cols), lambda i: (0, 0)),
            pl.BlockSpec((TILE, cols), lambda i: (top, 0)),
        ],
        out_specs=[whole, whole],
        out_shape=[jax.ShapeDtypeStruct((message, cols), f32)] * 2,
        name="row_pack",
    )(t, t, s, s, u, u, v, v, spacing_lengths, spacing_lengths, ocean_layer_number, ocean_layer_number)

    axes = ("lon", "lat")

    def place(lat, lon):
        return lon * lats + lat

    swap1, swap2 = [], []
    for lon in range(lons):
        for lat in range(0, lats, 2):
            swap1 += [(place(lat, lon), place(lat + 1, lon)), (place(lat + 1, lon), place(lat, lon))]
        for lat in range(1, lats - 1, 2):
            swap2 += [(place(lat, lon), place(lat + 1, lon)), (place(lat + 1, lon), place(lat, lon))]
        swap2.append((place(lats - 1, lon), place(lats - 1, lons - 1 - lon)))
    got1 = lax.ppermute(first, axes, swap1)
    got2 = lax.ppermute(second, axes, swap2)

    group = 8
    slab = pl.BlockSpec((group, rows, cols), lambda i: (i, 0, 0))
    message_out = jax.ShapeDtypeStruct((rows + 8, LANES), f32)
    to_east, to_west = pl.pallas_call(
        lambda *refs: column_pack(group, *refs),
        grid=(levels // group,),
        in_specs=[slab] * 4
        + [pl.BlockSpec((2, rows, cols), lambda i: (1, 0, 0)), pl.BlockSpec((rows, cols), lambda i: (0, 0))],
        out_specs=[pl.BlockSpec((rows + 8, LANES), lambda i: (0, 0))] * 2,
        out_shape=[message_out] * 2,
        compiler_params=pltpu.CompilerParams(vmem_limit_bytes=60 * 2**20),
        cost_estimate=pl.CostEstimate(flops=20 * t.size, bytes_accessed=16 * t.size, transcendentals=0),
        name="column_pack",
    )(t, s, u, v, spacing_lengths, ocean_layer_number)

    seam = seam_partner_index.reshape(-1, LANES)
    fixed = lambda *shape: pl.BlockSpec(shape, lambda i: (0,) * len(shape))
    high_edge = pl.BlockSpec((8, LANES), lambda i: (rows // 8, 0))
    low_edge = pl.BlockSpec((8, LANES), lambda i: (0, 0))
    tight = pltpu.CompilerParams(vmem_limit_bytes=60 * 2**20)
    u_rows = pl.BlockSpec((levels, cols), lambda i: (ZONAL, 0))
    v_rows = pl.BlockSpec((levels, cols), lambda i: (MERID, 0))
    to_east, to_west = pl.pallas_call(
        corners,
        grid=(1,),
        in_specs=[u_rows, u_rows, v_rows, v_rows, fixed(*seam.shape), high_edge, low_edge],
        out_specs=[high_edge, low_edge],
        out_shape=[message_out] * 2,
        input_output_aliases={5: 0, 6: 1},
        compiler_params=tight,
        name="corners",
    )(got1, got2, got1, got2, seam, to_east, to_west)

    from_west = lax.ppermute(to_east, "lon", [(i, (i + 1) % lons) for i in range(lons)])
    from_east = lax.ppermute(to_west, "lon", [((i + 1) % lons, i) for i in range(lons)])

    north, south = pl.pallas_call(
        halo_rows,
        grid=(1,),
        in_specs=[fixed(message, cols)] * 4 + [fixed(*seam.shape)],
        out_specs=[fixed(message, cols), fixed(4 * levels, cols)],
        out_shape=[jax.ShapeDtypeStruct((message, cols), f32), jax.ShapeDtypeStruct((4 * levels, cols), f32)],
        compiler_params=tight,
        cost_estimate=pl.CostEstimate(flops=4 * t.size, bytes_accessed=2 * t.size, transcendentals=0),
        name="halo_rows",
    )(first, second, got1, got2, seam)

    halves = cols // LANES
    held = (halves, levels, rows + 2 * TILE, LANES)
    anywhere = pl.BlockSpec(memory_space=pl.ANY)
    out = jax.ShapeDtypeStruct((levels, rows, cols), f32)
    return pl.pallas_call(
        step_kernel,
        in_specs=[anywhere] * 12,
        out_specs=[anywhere] * 3,
        out_shape=[out] * 3,
        scratch_shapes=[
            pltpu.VMEM((message, cols), f32),
            pltpu.VMEM((4 * levels, cols), f32),
        ]
        + [pltpu.VMEM((rows + 8, LANES), f32)] * 3
        + [pltpu.VMEM(held, f32)] * 6
        + [
            pltpu.VMEM((5, halves, levels, TILE, LANES), f32),
            pltpu.VMEM((halves, levels, 2 * TILE, LANES), f32),
            pltpu.VMEM((halves, levels, 2 * TILE, LANES), f32),
        ]
        * 2
        + [
            pltpu.VMEM(spacing_lengths.shape, f32),
            pltpu.VMEM(planetary_spin.shape, f32),
            pltpu.VMEM((rows, cols), jnp.int32),
            pltpu.VMEM((halves, rows + TILE, LANES), f32),
        ]
        + [pltpu.VMEM((levels, rows, cols), f32)] * 3
        + [
            pltpu.VMEM((3, cols, cols), jnp.bfloat16),
            pltpu.VMEM((3, cols, cols), jnp.bfloat16),
            pltpu.VMEM((4, levels // 2, 2 * TILE, LANES), jnp.bfloat16),
            pltpu.SemaphoreType.DMA((rows // TILE // 2 + 1,)),
            pltpu.SemaphoreType.DMA((8,)),
            pltpu.SemaphoreType.DMA((3,)),
        ],
        compiler_params=pltpu.CompilerParams(vmem_limit_bytes=60 * 2**20),
        name="ocean_step",
    )(t, s, u, v, spacing_lengths, planetary_spin, ocean_layer_number, north, south, to_west, from_east, from_west)


def solution(mesh):
    in_specs = (
        P(None, "lat", "lon"),
        P(None, "lat", "lon"),
        P(None, "lat", "lon"),
        P(None, "lat", "lon"),
        P(None, "lat", "lon"),
        P(None, "lat", "lon"),
        P("lat", "lon"),
        P(),
    )
    out_specs = (P(None, "lat", "lon"), P(None, "lat", "lon"), P(None, "lat", "lon"))
    return jax.shard_map(body, mesh=mesh, in_specs=in_specs, out_specs=out_specs, check_vma=False)
```

time: 54.5 us -> 44.7 us (0.82)
  waiting for transfers between devices: 10 us -> 3.15 us
  Pallas kernels: 33 us -> 30.5 us
    ppermute x1, waiting for transfers between devices: 4.79 us -> 0.01 us  [body(): got2 = lax.ppermute(second, axes, swap2)]
    pallas_call x1, Pallas kernels: 7.75 us -> 5.39 us  [body(): pl.pallas_call(lambda *refs: column_pack(group, *refs), grid=(levels // g...]
    ppermute x1, waiting for transfers between devices: 2.19 us -> 0.37 us  [body(): lax.ppermute(to_east, 'lon', [(i, (i + 1) % lons) for i in range(lons)])]
    pallas_call x1 -> x3, Pallas kernels: 23.2 us -> 23 us  [the longest x1 19.6 us: body(): pl.pallas_call(step_kernel, in_specs=[anywhere] * 12, out_specs=[anywhere...]
  transfers between devices with their start and end apart: 4 -> 4, of which waited for: 4 -> 2; matrix products, arithmetic and copies ran while one was open for 0% -> 0% of each run, Pallas kernels for 0% -> 16%
where the time goes in v1:
time: 44.7 us; the launch traced here: 44.5 us
  Pallas kernels  30.5 us (68%)
  starting transfers between devices  8.87 us (20%)
  waiting for transfers between devices  3.15 us (7%)
  local copies, waits for them, and re-layouts  1.27 us (3%)
  between operations  0.67 us (1%)
    pallas_call x1, Pallas kernels, body(): pl.pallas_call(step_kernel, in_specs=[anywhere] * 12, out_specs=[anywhere...  19.6 us
    pallas_call x1, Pallas kernels, body(): pl.pallas_call(lambda *refs: column_pack(group, *refs), grid=(levels // g...  5.39 us
    ppermute x1, starting transfers between devices, body(): lax.ppermute(to_east, 'lon', [(i, (i + 1) % lons) for i in range(lons)])  4.03 us
    ppermute x1, starting transfers between devices, body(): got2 = lax.ppermute(second, axes, swap2)  2.82 us
    ppermute x1, waiting for transfers between devices, body(): lax.ppermute(to_west, 'lon', [((i + 1) % lons, i) for i in range(lons)])  2.78 us
    pallas_call x1, Pallas kernels, body(): pl.pallas_call(row_pack, grid=(1,), in_specs=[low3, high3] * 4 + [pl.Bloc...  2.09 us
    ppermute x1, starting transfers between devices, body(): got1 = lax.ppermute(first, axes, swap1)  2.02 us
    pallas_call x1, Pallas kernels, body(): pl.pallas_call(halo_rows, grid=(1,), in_specs=[fixed(message, cols)] * 4...  1.82 us
  transfers between devices with their start and end apart: 4, of which 2 were waited for; matrix products, arithmetic and copies ran while one was open for 0% of the time, Pallas kernels for 16%

profile of v1, /device:TPU:13, one launch (start us, length us, event | category | flops | bytes accessed | tf_op | source)
XLA Modules:
  0.0 44.5 jit_solution(15963786909495648272)
XLA Ops:
  0.6 2.1 %row_pack.1 = (f32[88,256]{1,0:T(8,128)}, f32[88,256]{1,0:T(8,128)}) custom-call(f32[16,152,256]{2,1,0:T(8,128)} %t_hbm.1, f32[16,152,256]{2,1,0:T(8,128)} %t_hbm.1, f32[16,152,256]{2,1,0:T(8,128)} %s_hbm.1, f32[16,152,256]{2,1,0:T(8,128)} %s_hbm.1, f32[16,152,256]{2,1,0:T(8,128)} %u_hbm.1, f32[16,152,256]{2,1,0:T(8,128)} %u_hbm.1, f32[16,152,256]{2,1,0:T(8,128)} %v_hbm.1, ...), custom_call_target="tpu_custom_call" | custom-call | tf_op jit(solution)/shard_map/row_pack/pallas_call | solution.py:614
  2.7 2.0 %collective-permute-start = (f32[88,256]{1,0:T(8,128)}, f32[88,256]{1,0:T(8,128)S(1)}, u32[]{:S(2)}, u32[]{:S(2)}) collective-permute-start(f32[88,256]{1,0:T(8,128)} %get-tuple-element.11.mine1), channel_id=1, source_target_pairs={{0,1},{1,0},{2,3},{3,2},{4,5},{5,4},{6,7},{7,6},{8,9},{9,8},{10,11... | collective-permute-start | bytes 270344 | tf_op jit(solution)/shard_map/ppermute | solution.py:641
  4.7 2.8 %collective-permute-start.1 = (f32[88,256]{1,0:T(8,128)}, f32[88,256]{1,0:T(8,128)S(1)}, u32[]{:S(2)}, u32[]{:S(2)}) collective-permute-start(f32[88,256]{1,0:T(8,128)} %get-tuple-element.12.mine2), channel_id=1, source_target_pairs={{1,2},{2,1},{3,4},{4,3},{5,6},{6,5},{7,127},{9,10},{10,9},{11,12},... | collective-permute-start | bytes 270344 | tf_op jit(solution)/shard_map/ppermute | solution.py:642
  7.6 5.4 %column_pack.1 = (f32[160,128]{1,0:T(8,128)}, f32[160,128]{1,0:T(8,128)}) custom-call(f32[16,152,256]{2,1,0:T(8,128)} %t_hbm.1, f32[16,152,256]{2,1,0:T(8,128)} %s_hbm.1, f32[16,152,256]{2,1,0:T(8,128)} %u_hbm.1, f32[16,152,256]{2,1,0:T(8,128)} %v_hbm.1, f32[6,152,256]{2,1,0:T(8,128)} %e_hbm.1, s32[152,256]{1,0:T(8,128)} %n_hbm.1), custom_call_target="tpu_custom_call" | custom-call | flops 12451840 | bytes 9961472 | tf_op jit(solution)/shard_map/column_pack/pallas_call | solution.py:647
  13.0 0.0 collective-permute-done.got1.u1.v1
  13.0 0.0 copy-start
  13.0 0.0 collective-permute-done.1.got2.u2.v2
  13.0 0.0 copy-start.1
  13.0 0.6 %copy-done = f32[88,256]{1,0:T(8,128)} copy-done((f32[88,256]{1,0:T(8,128)}, f32[88,256]{1,0:T(8,128)S(1)}, u32[]{:S(2)}) %copy-start) | copy-done | bytes 90136
  13.6 0.0 copy-done.1
  13.6 1.6 %corners.1 = (f32[160,128]{1,0:T(8,128)}, f32[160,128]{1,0:T(8,128)}) custom-call(f32[88,256]{1,0:T(8,128)} %copy-done, f32[88,256]{1,0:T(8,128)} %copy-done.1, f32[88,256]{1,0:T(8,128)} %copy-done, f32[88,256]{1,0:T(8,128)} %copy-done.1, s32[32,128]{1,0:T(8,128)} %bitcast.1, ...), custom_call_target="tpu_custom_call", output_to_operand_aliasing={{0}: (5, {}), {1}: (6, {})} | custom-call | tf_op jit(solution)/shard_map/corners/pallas_call | solution.py:666
  15.2 4.0 %collective-permute-start.3 = (f32[160,128]{1,0:T(8,128)}, f32[160,128]{1,0:T(8,128)S(1)}, u32[]{:S(2)}, u32[]{:S(2)}) collective-permute-start(f32[160,128]{1,0:T(8,128)} %get-tuple-element.18), channel_id=1, source_target_pairs={{0,8},{8,16},{16,24},{24,32},{32,40},{40,48},{48,56},{56,64},{64,7... | collective-permute-start | bytes 245768 | tf_op jit(solution)/shard_map/ppermute | solution.py:677
  19.2 0.0 collective-permute-start.2
  19.2 1.8 %halo_rows.1 = (f32[88,256]{1,0:T(8,128)}, f32[64,256]{1,0:T(8,128)}) custom-call(f32[88,256]{1,0:T(8,128)} %get-tuple-element.11.mine1, f32[88,256]{1,0:T(8,128)} %get-tuple-element.12.mine2, f32[88,256]{1,0:T(8,128)} %copy-done, f32[88,256]{1,0:T(8,128)} %copy-done.1, s32[32,128]{1,0:T(8,128)} %bitcast.2), custom_call_target="tpu_custom_call" | custom-call | flops 2490368 | bytes 1245184 | tf_op jit(solution)/shard_map/halo_rows/pallas_call | solution.py:680
  21.1 0.4 collective-permute-done.3.from_west_hbm
  21.4 0.0 copy-start.2
  21.4 2.8 %collective-permute-done.2.from_east_hbm = f32[160,128]{1,0:T(8,128)S(1)} collective-permute-done((f32[160,128]{1,0:T(8,128)}, f32[160,128]{1,0:T(8,128)S(1)}, u32[]{:S(2)}, u32[]{:S(2)}) %collective-permute-start.2) | collective-permute-done | bytes 81952 | tf_op jit(solution)/shard_map/ppermute | solution.py:678
  24.2 0.0 copy-start.3
  24.2 0.0 copy-done.2
  24.2 0.6 %copy-done.3 = f32[160,128]{1,0:T(8,128)} copy-done((f32[160,128]{1,0:T(8,128)}, f32[160,128]{1,0:T(8,128)S(1)}, u32[]{:S(2)}) %copy-start.3) | copy-done | bytes 81944
  24.9 19.6 %ocean_step.1 = (f32[16,152,256]{2,1,0:T(8,128)}, f32[16,152,256]{2,1,0:T(8,128)}, f32[16,152,256]{2,1,0:T(8,128)}) custom-call(f32[16,152,256]{2,1,0:T(8,128)} %t_hbm.1, f32[16,152,256]{2,1,0:T(8,128)} %s_hbm.1, f32[16,152,256]{2,1,0:T(8,128)} %u_hbm.1, f32[16,152,256]{2,1,0:T(8,128)} %v_hbm.1, f32[6,152,256]{2,1,0:T(8,128)} %e_hbm.1, ...), custom_call_target="tpu_custom_call" | custom-call | tf_op jit(solution)/shard_map/ocean_step/pallas_call | solution.py:695
Async XLA Ops:
  2.7 10.2 %collective-permute-start = (f32[88,256]{1,0:T(8,128)}, f32[88,256]{1,0:T(8,128)S(1)}, u32[]{:S(2)}, u32[]{:S(2)}) collective-permute-start(f32[88,256]{1,0:T(8,128)} %get-tuple-element.11.mine1), channel_id=1, source_target_pairs={{0,1},{1,0},{2,3},{3,2},{4,5},{5,4},{6,7},{7,6},{8,9},{9,8},{10,11... | collective-permute-start | bytes 270344 | tf_op jit(solution)/shard_map/ppermute | solution.py:641
  4.7 8.2 %collective-permute-start.1 = (f32[88,256]{1,0:T(8,128)}, f32[88,256]{1,0:T(8,128)S(1)}, u32[]{:S(2)}, u32[]{:S(2)}) collective-permute-start(f32[88,256]{1,0:T(8,128)} %get-tuple-element.12.mine2), channel_id=1, source_target_pairs={{1,2},{2,1},{3,4},{4,3},{5,6},{6,5},{7,127},{9,10},{10,9},{11,12},... | collective-permute-start | bytes 270344 | tf_op jit(solution)/shard_map/ppermute | solution.py:642
  13.0 0.6 %copy-start = (f32[88,256]{1,0:T(8,128)}, f32[88,256]{1,0:T(8,128)S(1)}, u32[]{:S(2)}) copy-start(f32[88,256]{1,0:T(8,128)S(1)} %collective-permute-done.got1.u1.v1) | copy-start | bytes 270340
  13.0 0.6 %copy-start.1 = (f32[88,256]{1,0:T(8,128)}, f32[88,256]{1,0:T(8,128)S(1)}, u32[]{:S(2)}) copy-start(f32[88,256]{1,0:T(8,128)S(1)} %collective-permute-done.1.got2.u2.v2) | copy-start | bytes 270340
  15.2 6.2 %collective-permute-start.3 = (f32[160,128]{1,0:T(8,128)}, f32[160,128]{1,0:T(8,128)S(1)}, u32[]{:S(2)}, u32[]{:S(2)}) collective-permute-start(f32[160,128]{1,0:T(8,128)} %get-tuple-element.18), channel_id=1, source_target_pairs={{0,8},{8,16},{16,24},{24,32},{32,40},{40,48},{48,56},{56,64},{64,7... | collective-permute-start | bytes 245768 | tf_op jit(solution)/shard_map/ppermute | solution.py:677
  19.2 5.0 %collective-permute-start.2 = (f32[160,128]{1,0:T(8,128)}, f32[160,128]{1,0:T(8,128)S(1)}, u32[]{:S(2)}, u32[]{:S(2)}) collective-permute-start(f32[160,128]{1,0:T(8,128)} %get-tuple-element.17.own_hbm), channel_id=1, source_target_pairs={{8,0},{16,8},{24,16},{32,24},{40,32},{48,40},{56,48},{64,56},{72,6... | collective-permute-start | bytes 245768 | tf_op jit(solution)/shard_map/ppermute | solution.py:678
  21.4 2.8 %copy-start.2 = (f32[160,128]{1,0:T(8,128)}, f32[160,128]{1,0:T(8,128)S(1)}, u32[]{:S(2)}) copy-start(f32[160,128]{1,0:T(8,128)S(1)} %collective-permute-done.3.from_west_hbm) | copy-start | bytes 245764
  24.2 0.6 %copy-start.3 = (f32[160,128]{1,0:T(8,128)}, f32[160,128]{1,0:T(8,128)S(1)}, u32[]{:S(2)}) copy-start(f32[160,128]{1,0:T(8,128)S(1)} %collective-permute-done.2.from_east_hbm) | copy-start | bytes 245764

commit v2 on v1

--- a/solution.py
+++ b/solution.py
@@ -174,7 +174,7 @@
 def step_kernel(
     t_hbm, s_hbm, u_hbm, v_hbm, e_hbm, f_hbm, n_hbm, north_hbm, south_hbm, own_hbm, from_east_hbm, from_west_hbm,
     u_out, v_out, t_out,
-    north, south, own_west, from_east, from_west, t_s, s_s, u_s, v_s, d_s, g_s, mixed_a, uw_a, ve_a, mixed_b, uw_b, ve_b, e_s, f_s, n_s, nf_s, uo_s, vo_s, to_s, move_s, rim_s, mask_s,
+    north, south, own_west, from_east, from_west, t_s, s_s, u_s, v_s, d_s, g_s, mixed_a, uw_a, ve_a, mixed_b, uw_b, ve_b, e_s, f_s, n_s, nf_s, uo_s, vo_s, to_s, move_s, rim_s, mask_s, coef_s,
     in_sem, flat_sem, out_sem,
 ):
     levels, rows, cols = t_hbm.shape
@@ -224,9 +224,9 @@
     for copy in flat[2:]:
         copy.start()
     load(0, 1, 0)
+    for copy in flat[:2]:
+        copy.start()
     load(1, 2, 1)
-    flat[0].start()
-    flat[1].start()
     for unit in range(2, pairs + 1):
         load(2 * unit - 1, 2, unit)
 
@@ -283,8 +283,6 @@
         nf_s[h, rows : rows + 1, :] = north[5 * levels + WET_AT : 5 * levels + WET_AT + 1, span]
     for h in both:
         nf_s[h, 0:rows, :] = n_s[:, h * LANES : (h + 1) * LANES].astype(jnp.float32)
-    loaded(1, 0)
-    loaded(2, 1)
 
     lane = lax.broadcasted_iota(jnp.int32, (TILE, LANES), 1)
     is_last = lane == LANES - 1
@@ -341,9 +339,31 @@
             y = y + jnp.dot(p, move_s[i], preferred_element_type=jnp.float32)
         return y
 
+    def prepare(r):
+        flat_at = pl.ds(pl.multiple_of(r * TILE, TILE), TILE)
+        dt = step_duration
+        wet = [nf_s[h, flat_at, :] for h in both]
+        wet_e = east_of(wet, from_east[pl.ds(pl.multiple_of(r * TILE, TILE) + TILE, TILE), :], WET_LANE)
+        for h in both:
+            e1t, e2t, e1u, e2u, e1v, e2v = (e_s[i, flat_at, h * LANES : (h + 1) * LANES] for i in range(6))
+            fu, fv = (f_s[i, flat_at, h * LANES : (h + 1) * LANES] for i in range(2))
+            wet_n = nf_s[h, pl.ds(pl.multiple_of(r * TILE, TILE) + 1, TILE), :]
+            iu1, iu2, iv1, iv2 = (inverse_of(x) for x in (e1u, e2u, e1v, e2v))
+
+            def speeds(spin, along, across, a, b):
+                c4, c5 = dt * viscosity * a * a, dt * viscosity * b * b
+                return 0.25 * dt * spin, 0.125 * dt * across, 0.5 * dt * along, c4, c5, 2.0 * (c4 + c5)
+
+            values = speeds(fu, iu1, iu2, iu1, iu2) + (0.5 * gravity * dt * iu1, diffusivity * e2u * iu1, e2u * (1.0 / 12.0))
+            values += speeds(-fv, iv2, iv1, iv1, iv2) + (0.5 * gravity * dt * iv2, diffusivity * e1v * iv2, e1v * (1.0 / 12.0))
+            values += (dt * inverse_of(e1t * e2t), jnp.minimum(wet[h], wet_e[h]), jnp.minimum(wet[h], wet_n))
+            for i, value in enumerate(values):
+                coef_s[i, h, flat_at, :] = value
+
     def mix(r, kept, previous):
         mixed, uw_s, ve_s = kept
         row = pl.multiple_of(r * TILE, TILE)
+        prepare(r)
 
         def turned(x, order):
             return jnp.take_along_axis(x, order, axis=1, mode="promise_in_bounds")
@@ -439,33 +459,8 @@
         flux_w = flux_w - e2 * (1.0 / 12.0) * to_lane(west, ZONAL_LANE, 0) * (7.0 * t_sum - t_far)
         flux_w = jnp.where(lane.astype(jnp.float32) < wet_w, flux_w, 0.0)
 
-        def flat_of(ref, i):
-            return [ref[i, flat_at, h * LANES : (h + 1) * LANES] for h in both]
-
-        e1t, e2t, e1u, e2u, e1v, e2v = (flat_of(e_s, i) for i in range(6))
-        fu, fv = flat_of(f_s, 0), flat_of(f_s, 1)
-        wet = [nf_s[h, flat_at, :] for h in both]
-        wet_n = [nf_s[h, pl.ds(row + 1, TILE), :] for h in both]
-        wet_e = east_of(wet, east, WET_LANE)
-        u_wet = [jnp.minimum(wet[h], wet_e[h]) for h in both]
-        v_wet = [jnp.minimum(wet[h], wet_n[h]) for h in both]
-        dt = step_duration
-        area = [dt * inverse_of(e1t[h] * e2t[h]) for h in both]
-
-        def speeds(spin, along, across, a, b):
-            c4, c5 = dt * viscosity * a * a, dt * viscosity * b * b
-            return 0.25 * dt * spin, 0.125 * dt * across, 0.5 * dt * along, c4, c5, 2.0 * (c4 + c5)
-
-        iu1, iu2 = [inverse_of(x) for x in e1u], [inverse_of(x) for x in e2u]
-        iv1, iv2 = [inverse_of(x) for x in e1v], [inverse_of(x) for x in e2v]
-        iso_e = [diffusivity * e2u[h] * iu1[h] for h in both]
-        adv_e = [e2u[h] * (1.0 / 12.0) for h in both]
-        iso_n = [diffusivity * e1v[h] * iv2[h] for h in both]
-        adv_n = [e1v[h] * (1.0 / 12.0) for h in both]
-        cu = [speeds(fu[h], iu1[h], iu2[h], iu1[h], iu2[h]) for h in both]
-        cv = [speeds(-fv[h], iv2[h], iv1[h], iv1[h], iv2[h]) for h in both]
-        pu = [0.5 * gravity * dt * iu1[h] for h in both]
-        pv = [0.5 * gravity * dt * iv2[h] for h in both]
+        def coefficient(i):
+            return [coef_s[i, h, flat_at, :] for h in both]
 
         store_at = lambda h: (flat_at, pl.ds(h * LANES, LANES))
         zero = jnp.zeros((TILE, LANES), jnp.float32)
@@ -481,6 +476,8 @@
             vbar = [
                 (v[h] + vs[h]) + (ve_s[h, k, TILE : 2 * TILE, :] + ve_s[h, k, TILE - 1 : 2 * TILE - 1, :]) for h in both
             ]
+            c1, c2, c3, c4, c5, c6, pu, iso_e, adv_e = (coefficient(i) for i in range(9))
+            u_wet = coefficient(19)
             out = []
             for h in both:
                 rise = de[h] - d[h]
@@ -488,12 +485,11 @@
                 out.append((t[h] + te[h], d[h] + de[h], direct, iso_e[h] * rise))
                 press = run[h] + rise
                 run[h] = press + rise
-                c1, c2, c3, c4, c5, c6 = cu[h]
                 du = (
-                    vbar[h] * (c1 - c2 * (un[h] - us[h]))
-                    - u[h] * (c3 * (ue[h] - uw[h]) + c6)
-                    + c4 * (ue[h] + uw[h])
-                    + c5 * (un[h] + us[h])
+                    vbar[h] * (c1[h] - c2[h] * (un[h] - us[h]))
+                    - u[h] * (c3[h] * (ue[h] - uw[h]) + c6[h])
+                    + c4[h] * (ue[h] + uw[h])
+                    + c5[h] * (un[h] + us[h])
                     - pu[h] * press
                 )
                 uo_s[(k,) + store_at(h)] = u[h] + jnp.where(u_wet[h] > k, du, 0.0)
@@ -505,6 +501,7 @@
             return jnp.where(open_face, flux, 0.0)
 
         def east_finish(k, below, here, above):
+            u_wet = coefficient(19)
             fe = [flux_of(below[h], here[h], above[h], u_wet[h] > k) for h in both]
             fw = west_of(fe, flux_w, k)
             for h in both:
@@ -526,6 +523,8 @@
             ve, vw = [ve_s[h, k, TILE : 2 * TILE, :] for h in both], [mixed[1, h, k] for h in both]
             u, un = rows_of(u_s, k, 0), rows_of(u_s, k, 1)
             ubar = [(u[h] + un[h]) + (uw_s[h, k, 0:TILE, :] + uw_s[h, k, 1 : TILE + 1, :]) for h in both]
+            c1, c2, c3, c4, c5, c6, pv, iso_n, adv_n = (coefficient(i) for i in range(9, 18))
+            v_wet = coefficient(20)
             out = []
             for h in both:
                 rise, pair = dn[h] - d[h], t[h] + tn[h]
@@ -533,18 +532,18 @@
                 out.append((pair, d[h] + dn[h], direct, iso_n[h] * rise))
                 press = run[h] + rise
                 run[h] = press + rise
-                c1, c2, c3, c4, c5, c6 = cv[h]
                 dv = (
-                    ubar[h] * (c1 - c2 * (ve[h] - vw[h]))
-                    - v[h] * (c3 * (vn[h] - vs[h]) + c6)
-                    + c4 * (ve[h] + vw[h])
-                    + c5 * (vn[h] + vs[h])
+                    ubar[h] * (c1[h] - c2[h] * (ve[h] - vw[h]))
+                    - v[h] * (c3[h] * (vn[h] - vs[h]) + c6[h])
+                    + c4[h] * (ve[h] + vw[h])
+                    + c5[h] * (vn[h] + vs[h])
                     - pv[h] * press
                 )
                 vo_s[(k,) + store_at(h)] = v[h] + jnp.where(v_wet[h] > k, dv, 0.0)
             return out
 
         def north_finish(k, below, here, above):
+            area, v_wet, wet = coefficient(18), coefficient(20), [nf_s[h, flat_at, :] for h in both]
             for h in both:
                 fn = flux_of(below[h], here[h], above[h], v_wet[h] > k)
                 g_s[h, k, pl.ds(row + TILE, TILE), :] = fn
@@ -561,9 +560,11 @@
         north_finish(levels - 1, below, here, here)
 
     set_a, set_b = (mixed_a, uw_a, ve_a), (mixed_b, uw_b, ve_b)
-    mix(0, set_a, set_b)
     flat[0].wait()
     flat[1].wait()
+    loaded(1, 0)
+    loaded(2, 1)
+    mix(0, set_a, set_b)
 
     def two_tiles(i, carry):
         @pl.when(i + 2 <= pairs)
@@ -651,7 +652,7 @@
         + [pl.BlockSpec((2, rows, cols), lambda i: (1, 0, 0)), pl.BlockSpec((rows, cols), lambda i: (0, 0))],
         out_specs=[pl.BlockSpec((rows + 8, LANES), lambda i: (0, 0))] * 2,
         out_shape=[message_out] * 2,
-        compiler_params=pltpu.CompilerParams(vmem_limit_bytes=60 * 2**20),
+        compiler_params=pltpu.CompilerParams(vmem_limit_bytes=64 * 2**20),
         cost_estimate=pl.CostEstimate(flops=20 * t.size, bytes_accessed=16 * t.size, transcendentals=0),
         name="column_pack",
     )(t, s, u, v, spacing_lengths, ocean_layer_number)
@@ -660,7 +661,7 @@
     fixed = lambda *shape: pl.BlockSpec(shape, lambda i: (0,) * len(shape))
     high_edge = pl.BlockSpec((8, LANES), lambda i: (rows // 8, 0))
     low_edge = pl.BlockSpec((8, LANES), lambda i: (0, 0))
-    tight = pltpu.CompilerParams(vmem_limit_bytes=60 * 2**20)
+    tight = pltpu.CompilerParams(vmem_limit_bytes=64 * 2**20)
     u_rows = pl.BlockSpec((levels, cols), lambda i: (ZONAL, 0))
     v_rows = pl.BlockSpec((levels, cols), lambda i: (MERID, 0))
     to_east, to_west = pl.pallas_call(
@@ -720,6 +721,7 @@
             pltpu.VMEM((3, cols, cols), jnp.bfloat16),
             pltpu.VMEM((3, cols, cols), jnp.bfloat16),
             pltpu.VMEM((4, levels // 2, 2 * TILE, LANES), jnp.bfloat16),
+            pltpu.VMEM((21, halves, rows, LANES), f32),
             pltpu.SemaphoreType.DMA((rows // TILE // 2 + 1,)),
             pltpu.SemaphoreType.DMA((8,)),
             pltpu.SemaphoreType.DMA((3,)),

time: 44.7 us -> 43.6 us (0.975)
  local copies, waits for them, and re-layouts: 1.27 us -> 0 us
    unnamed x8 -> x0, local copies, waits for them, and re-layouts: 1.27 us -> none
  transfers between devices with their start and end apart: 4 -> 4, of which waited for: 2 -> 2; matrix products, arithmetic and copies ran while one was open for 0% -> 0% of each run, Pallas kernels for 16% -> 17%
where the time goes in v2:
time: 43.6 us; the launch traced here: 43.3 us
  Pallas kernels  30.4 us (70%)
  starting transfers between devices  8.99 us (21%)
  waiting for transfers between devices  3.28 us (8%)
  between operations  0.65 us (1%)
    pallas_call x1, Pallas kernels, body(): pl.pallas_call(step_kernel, in_specs=[anywhere] * 12, out_specs=[anywhere...  19.5 us
    pallas_call x1, Pallas kernels, body(): pl.pallas_call(lambda *refs: column_pack(group, *refs), grid=(levels // g...  5.4 us
    ppermute x1, starting transfers between devices, body(): lax.ppermute(to_east, 'lon', [(i, (i + 1) % lons) for i in range(lons)])  4.15 us
    ppermute x1, waiting for transfers between devices, body(): lax.ppermute(to_west, 'lon', [((i + 1) % lons, i) for i in range(lons)])  2.88 us
    ppermute x1, starting transfers between devices, body(): got2 = lax.ppermute(second, axes, swap2)  2.82 us
    pallas_call x1, Pallas kernels, body(): pl.pallas_call(row_pack, grid=(1,), in_specs=[low3, high3] * 4 + [pl.Bloc...  2.09 us
    ppermute x1, starting transfers between devices, body(): got1 = lax.ppermute(first, axes, swap1)  2.02 us
    pallas_call x1, Pallas kernels, body(): pl.pallas_call(halo_rows, grid=(1,), in_specs=[fixed(message, cols)] * 4...  1.8 us
  transfers between devices with their start and end apart: 4, of which 2 were waited for; matrix products, arithmetic and copies ran while one was open for 0% of the time, Pallas kernels for 17%

profile of v2, /device:TPU:13, one launch (start us, length us, event | category | flops | bytes accessed | tf_op | source)
XLA Modules:
  0.0 43.3 jit_solution(11292154684141835961)
XLA Ops:
  0.6 2.1 %row_pack.1 = (f32[88,256]{1,0:T(8,128)}, f32[88,256]{1,0:T(8,128)}) custom-call(f32[16,152,256]{2,1,0:T(8,128)} %t_hbm.1, f32[16,152,256]{2,1,0:T(8,128)} %t_hbm.1, f32[16,152,256]{2,1,0:T(8,128)} %s_hbm.1, f32[16,152,256]{2,1,0:T(8,128)} %s_hbm.1, f32[16,152,256]{2,1,0:T(8,128)} %u_hbm.1, f32[16,152,256]{2,1,0:T(8,128)} %u_hbm.1, f32[16,152,256]{2,1,0:T(8,128)} %v_hbm.1, ...), custom_call_target="tpu_custom_call" | custom-call | tf_op jit(solution)/shard_map/row_pack/pallas_call | solution.py:615
  2.7 2.0 %collective-permute-start = (f32[88,256]{1,0:T(8,128)}, f32[88,256]{1,0:T(8,128)}, u32[]{:S(2)}, u32[]{:S(2)}) collective-permute-start(f32[88,256]{1,0:T(8,128)} %get-tuple-element.11.mine1), channel_id=1, source_target_pairs={{0,1},{1,0},{2,3},{3,2},{4,5},{5,4},{6,7},{7,6},{8,9},{9,8},{10,11... | collective-permute-start | bytes 270344 | tf_op jit(solution)/shard_map/ppermute | solution.py:642
  4.7 2.8 %collective-permute-start.1 = (f32[88,256]{1,0:T(8,128)}, f32[88,256]{1,0:T(8,128)}, u32[]{:S(2)}, u32[]{:S(2)}) collective-permute-start(f32[88,256]{1,0:T(8,128)} %get-tuple-element.12.mine2), channel_id=1, source_target_pairs={{1,2},{2,1},{3,4},{4,3},{5,6},{6,5},{7,127},{9,10},{10,9},{11,12},... | collective-permute-start | bytes 270344 | tf_op jit(solution)/shard_map/ppermute | solution.py:643
  7.6 5.4 %column_pack.1 = (f32[160,128]{1,0:T(8,128)}, f32[160,128]{1,0:T(8,128)}) custom-call(f32[16,152,256]{2,1,0:T(8,128)} %t_hbm.1, f32[16,152,256]{2,1,0:T(8,128)} %s_hbm.1, f32[16,152,256]{2,1,0:T(8,128)} %u_hbm.1, f32[16,152,256]{2,1,0:T(8,128)} %v_hbm.1, f32[6,152,256]{2,1,0:T(8,128)} %e_hbm.1, s32[152,256]{1,0:T(8,128)} %n_hbm.1), custom_call_target="tpu_custom_call" | custom-call | flops 12451840 | bytes 9961472 | tf_op jit(solution)/shard_map/column_pack/pallas_call | solution.py:648
  13.0 0.0 collective-permute-done.got1.u1.v1
  13.0 0.0 collective-permute-done.1.got2.u2.v2
  13.0 1.6 %corners.1 = (f32[160,128]{1,0:T(8,128)}, f32[160,128]{1,0:T(8,128)}) custom-call(f32[88,256]{1,0:T(8,128)} %collective-permute-done.got1.u1.v1, f32[88,256]{1,0:T(8,128)} %collective-permute-done.1.got2.u2.v2, f32[88,256]{1,0:T(8,128)} %collective-permute-done.got1.u1.v1, ...), custom_call_target="tpu_custom_call", output_to_operand_aliasing={{0}: (5, {}), {1}: (6, {})} | custom-call | tf_op jit(solution)/shard_map/corners/pallas_call | solution.py:667
  14.6 4.1 %collective-permute-start.3 = (f32[160,128]{1,0:T(8,128)}, f32[160,128]{1,0:T(8,128)}, u32[]{:S(2)}, u32[]{:S(2)}) collective-permute-start(f32[160,128]{1,0:T(8,128)} %get-tuple-element.18), channel_id=1, source_target_pairs={{0,8},{8,16},{16,24},{24,32},{32,40},{40,48},{48,56},{56,64},{64,7... | collective-permute-start | bytes 245768 | tf_op jit(solution)/shard_map/ppermute | solution.py:678
  18.7 0.0 collective-permute-start.2
  18.7 1.8 %halo_rows.1 = (f32[88,256]{1,0:T(8,128)}, f32[64,256]{1,0:T(8,128)}) custom-call(f32[88,256]{1,0:T(8,128)} %get-tuple-element.11.mine1, f32[88,256]{1,0:T(8,128)} %get-tuple-element.12.mine2, f32[88,256]{1,0:T(8,128)} %collective-permute-done.got1.u1.v1, f32[88,256]{1,0:T(8,128)} %collective-permute-done.1.got2.u2.v2, s32[32,128]{1,0:T(8,128)} %bitcast.2), custom_call_target="tpu_custom_call" | custom-call | flops 2490368 | bytes 1245184 | tf_op jit(solution)/shard_map/halo_rows/pallas_call | solution.py:681
  20.5 0.4 collective-permute-done.3.from_west_hbm
  20.9 2.9 %collective-permute-done.2.from_east_hbm = f32[160,128]{1,0:T(8,128)} collective-permute-done((f32[160,128]{1,0:T(8,128)}, f32[160,128]{1,0:T(8,128)}, u32[]{:S(2)}, u32[]{:S(2)}) %collective-permute-start.2) | collective-permute-done | bytes 81952 | tf_op jit(solution)/shard_map/ppermute | solution.py:679
  23.8 19.5 %ocean_step.1 = (f32[16,152,256]{2,1,0:T(8,128)}, f32[16,152,256]{2,1,0:T(8,128)}, f32[16,152,256]{2,1,0:T(8,128)}) custom-call(f32[16,152,256]{2,1,0:T(8,128)} %t_hbm.1, f32[16,152,256]{2,1,0:T(8,128)} %s_hbm.1, f32[16,152,256]{2,1,0:T(8,128)} %u_hbm.1, f32[16,152,256]{2,1,0:T(8,128)} %v_hbm.1, f32[6,152,256]{2,1,0:T(8,128)} %e_hbm.1, ...), custom_call_target="tpu_custom_call" | custom-call | tf_op jit(solution)/shard_map/ocean_step/pallas_call | solution.py:696
Async XLA Ops:
  2.7 10.3 %collective-permute-start = (f32[88,256]{1,0:T(8,128)}, f32[88,256]{1,0:T(8,128)}, u32[]{:S(2)}, u32[]{:S(2)}) collective-permute-start(f32[88,256]{1,0:T(8,128)} %get-tuple-element.11.mine1), channel_id=1, source_target_pairs={{0,1},{1,0},{2,3},{3,2},{4,5},{5,4},{6,7},{7,6},{8,9},{9,8},{10,11... | collective-permute-start | bytes 270344 | tf_op jit(solution)/shard_map/ppermute | solution.py:642
  4.7 8.2 %collective-permute-start.1 = (f32[88,256]{1,0:T(8,128)}, f32[88,256]{1,0:T(8,128)}, u32[]{:S(2)}, u32[]{:S(2)}) collective-permute-start(f32[88,256]{1,0:T(8,128)} %get-tuple-element.12.mine2), channel_id=1, source_target_pairs={{1,2},{2,1},{3,4},{4,3},{5,6},{6,5},{7,127},{9,10},{10,9},{11,12},... | collective-permute-start | bytes 270344 | tf_op jit(solution)/shard_map/ppermute | solution.py:643
  14.6 6.3 %collective-permute-start.3 = (f32[160,128]{1,0:T(8,128)}, f32[160,128]{1,0:T(8,128)}, u32[]{:S(2)}, u32[]{:S(2)}) collective-permute-start(f32[160,128]{1,0:T(8,128)} %get-tuple-element.18), channel_id=1, source_target_pairs={{0,8},{8,16},{16,24},{24,32},{32,40},{40,48},{48,56},{56,64},{64,7... | collective-permute-start | bytes 245768 | tf_op jit(solution)/shard_map/ppermute | solution.py:678
  18.7 5.1 %collective-permute-start.2 = (f32[160,128]{1,0:T(8,128)}, f32[160,128]{1,0:T(8,128)}, u32[]{:S(2)}, u32[]{:S(2)}) collective-permute-start(f32[160,128]{1,0:T(8,128)} %get-tuple-element.17.own_hbm), channel_id=1, source_target_pairs={{8,0},{16,8},{24,16},{32,24},{40,32},{48,40},{56,48},{64,56},{72,6... | collective-permute-start | bytes 245768 | tf_op jit(solution)/shard_map/ppermute | solution.py:679

commit v3 on v2

--- a/solution.py
+++ b/solution.py
@@ -174,7 +174,7 @@
 def step_kernel(
     t_hbm, s_hbm, u_hbm, v_hbm, e_hbm, f_hbm, n_hbm, north_hbm, south_hbm, own_hbm, from_east_hbm, from_west_hbm,
     u_out, v_out, t_out,
-    north, south, own_west, from_east, from_west, t_s, s_s, u_s, v_s, d_s, g_s, mixed_a, uw_a, ve_a, mixed_b, uw_b, ve_b, e_s, f_s, n_s, nf_s, uo_s, vo_s, to_s, move_s, rim_s, mask_s, coef_s,
+    north, south, own_west, from_east, from_west, t_s, s_s, u_s, v_s, g_s, mixed_a, uw_a, ve_a, den_a, coef_a, mixed_b, uw_b, ve_b, den_b, coef_b, e_s, f_s, n_s, nf_s, uo_s, vo_s, to_s, move_s, rim_s, mask_s,
     in_sem, flat_sem, out_sem,
 ):
     levels, rows, cols = t_hbm.shape
@@ -277,7 +277,6 @@
             v_s[h, k, low : low + 1, :] = south[3 * levels + k : 3 * levels + k + 1, span]
             t_s[h, k, high : high + 1, :] = north[NEAR * levels + k : NEAR * levels + k + 1, span]
             t_s[h, k, high + 1 : high + 2, :] = north[FAR * levels + k : FAR * levels + k + 1, span]
-            d_s[h, k, high : high + 1, :] = north_density[k : k + 1, span]
             u_s[h, k, high : high + 1, :] = north[ZONAL * levels + k : ZONAL * levels + k + 1, span]
             v_s[h, k, high : high + 1, :] = north[MERID * levels + k : MERID * levels + k + 1, span]
         nf_s[h, rows : rows + 1, :] = north[5 * levels + WET_AT : 5 * levels + WET_AT + 1, span]
@@ -339,7 +338,7 @@
             y = y + jnp.dot(p, move_s[i], preferred_element_type=jnp.float32)
         return y
 
-    def prepare(r):
+    def prepare(r, coef_s):
         flat_at = pl.ds(pl.multiple_of(r * TILE, TILE), TILE)
         dt = step_duration
         wet = [nf_s[h, flat_at, :] for h in both]
@@ -358,12 +357,12 @@
             values += speeds(-fv, iv2, iv1, iv1, iv2) + (0.5 * gravity * dt * iv2, diffusivity * e1v * iv2, e1v * (1.0 / 12.0))
             values += (dt * inverse_of(e1t * e2t), jnp.minimum(wet[h], wet_e[h]), jnp.minimum(wet[h], wet_n))
             for i, value in enumerate(values):
-                coef_s[i, h, flat_at, :] = value
+                coef_s[i, h] = value
 
     def mix(r, kept, previous):
-        mixed, uw_s, ve_s = kept
+        mixed, uw_s, ve_s, den_s, coef_s = kept
         row = pl.multiple_of(r * TILE, TILE)
-        prepare(r)
+        prepare(r, coef_s)
 
         def turned(x, order):
             return jnp.take_along_axis(x, order, axis=1, mode="promise_in_bounds")
@@ -391,7 +390,8 @@
 
         d = [density_of(salt, heat) for salt, heat in zip(held_in(s_s), held_in(t_s))]
         for h in both:
-            d_s[h, :, pl.ds(row + TILE, TILE), :] = d[h]
+            den_s[h, :, 0:TILE, :] = d[h]
+            previous[3][h, :, TILE : TILE + 1, :] = d[h][:, 0:1, :]
         parts = [of(held_in(u_s)), of(held_in(v_s)), of(held_in(t_s)), of(d)]
         y = moved([jnp.concatenate(p, axis=0) for p in zip(*parts)], jnp.concatenate([rim_u, rim_v, rim_t, rim_d], axis=0), 2)
         for h in both:
@@ -424,7 +424,7 @@
             ve_a[h, k, TILE - 1 : TILE, :] = edge[h][k : k + 1]
 
     def advance(r, kept, following):
-        mixed, uw_s, ve_s = kept
+        mixed, uw_s, ve_s, den_s, coef_s = kept
         for h in both:
             following[2][h, :, TILE - 1 : TILE, :] = ve_s[h, :, 2 * TILE - 1 : 2 * TILE, :]
         row = pl.multiple_of(r * TILE, TILE)
@@ -460,7 +460,7 @@
         flux_w = jnp.where(lane.astype(jnp.float32) < wet_w, flux_w, 0.0)
 
         def coefficient(i):
-            return [coef_s[i, h, flat_at, :] for h in both]
+            return [coef_s[i, h] for h in both]
 
         store_at = lambda h: (flat_at, pl.ds(h * LANES, LANES))
         zero = jnp.zeros((TILE, LANES), jnp.float32)
@@ -468,7 +468,8 @@
         run = [zero for _ in both]
 
         def east_parts(k):
-            t, d, u = rows_of(t_s, k, 0), rows_of(d_s, k, 0), rows_of(u_s, k, 0)
+            t, u = rows_of(t_s, k, 0), rows_of(u_s, k, 0)
+            d = [den_s[h, k, 0:TILE, :] for h in both]
             un, us = rows_of(u_s, k, 1), rows_of(u_s, k, -1)
             ue, wide, te, de = ([mixed[i, h, k] for h in both] for i in (0, 2, 3, 4))
             uw = [uw_s[h, k, 0:TILE, :] for h in both]
@@ -518,7 +519,7 @@
 
         def north_parts(k):
             t, tn, ts, tnn = (rows_of(t_s, k, i) for i in (0, 1, -1, 2))
-            d, dn = rows_of(d_s, k, 0), rows_of(d_s, k, 1)
+            d, dn = [den_s[h, k, 0:TILE, :] for h in both], [den_s[h, k, 1 : TILE + 1, :] for h in both]
             v, vn, vs = (rows_of(v_s, k, i) for i in (0, 1, -1))
             ve, vw = [ve_s[h, k, TILE : 2 * TILE, :] for h in both], [mixed[1, h, k] for h in both]
             u, un = rows_of(u_s, k, 0), rows_of(u_s, k, 1)
@@ -559,7 +560,7 @@
             below, here = here, above
         north_finish(levels - 1, below, here, here)
 
-    set_a, set_b = (mixed_a, uw_a, ve_a), (mixed_b, uw_b, ve_b)
+    set_a, set_b = (mixed_a, uw_a, ve_a, den_a, coef_a), (mixed_b, uw_b, ve_b, den_b, coef_b)
     flat[0].wait()
     flat[1].wait()
     loaded(1, 0)
@@ -585,6 +586,7 @@
     for h in both:
         for k in range(levels):
             uw_a[h, k, TILE : TILE + 1, :] = edge[h][k : k + 1]
+            den_a[h, k, TILE : TILE + 1, :] = north_density[k : k + 1, h * LANES : (h + 1) * LANES]
     advance(jnp.int32(2 * pairs), set_a, set_b)
     store(2 * pairs * TILE, 1)
     for i, (vmem, hbm) in enumerate(outs):
@@ -639,6 +641,7 @@
         for lat in range(1, lats - 1, 2):
             swap2 += [(place(lat, lon), place(lat + 1, lon)), (place(lat + 1, lon), place(lat, lon))]
         swap2.append((place(lats - 1, lon), place(lats - 1, lons - 1 - lon)))
+        swap2.append((place(0, lon), place(0, lon)))
     got1 = lax.ppermute(first, axes, swap1)
     got2 = lax.ppermute(second, axes, swap2)
 
@@ -703,11 +706,13 @@
             pltpu.VMEM((4 * levels, cols), f32),
         ]
         + [pltpu.VMEM((rows + 8, LANES), f32)] * 3
-        + [pltpu.VMEM(held, f32)] * 6
+        + [pltpu.VMEM(held, f32)] * 5
         + [
             pltpu.VMEM((5, halves, levels, TILE, LANES), f32),
             pltpu.VMEM((halves, levels, 2 * TILE, LANES), f32),
             pltpu.VMEM((halves, levels, 2 * TILE, LANES), f32),
+            pltpu.VMEM((halves, levels, 2 * TILE, LANES), f32),
+            pltpu.VMEM((21, halves, TILE, LANES), f32),
         ]
         * 2
         + [
@@ -721,7 +726,6 @@
             pltpu.VMEM((3, cols, cols), jnp.bfloat16),
             pltpu.VMEM((3, cols, cols), jnp.bfloat16),
             pltpu.VMEM((4, levels // 2, 2 * TILE, LANES), jnp.bfloat16),
-            pltpu.VMEM((21, halves, rows, LANES), f32),
             pltpu.SemaphoreType.DMA((rows // TILE // 2 + 1,)),
             pltpu.SemaphoreType.DMA((8,)),
             pltpu.SemaphoreType.DMA((3,)),

time: 43.6 us -> 43.7 us (level)
  no operation moved by 1% of the time
where the time goes in v3:
time: 43.7 us; the launch traced here: 43.4 us
  Pallas kernels  30.5 us (70%)
  starting transfers between devices  8.99 us (21%)
  waiting for transfers between devices  3.28 us (8%)
  between operations  0.65 us (1%)
    pallas_call x1, Pallas kernels, body(): pl.pallas_call(step_kernel, in_specs=[anywhere] * 12, out_specs=[anywhere...  19.6 us
    pallas_call x1, Pallas kernels, body(): pl.pallas_call(lambda *refs: column_pack(group, *refs), grid=(levels // g...  5.4 us
    ppermute x1, starting transfers between devices, body(): lax.ppermute(to_east, 'lon', [(i, (i + 1) % lons) for i in range(lons)])  4.15 us
    ppermute x1, waiting for transfers between devices, body(): lax.ppermute(to_west, 'lon', [((i + 1) % lons, i) for i in range(lons)])  2.88 us
    ppermute x1, starting transfers between devices, body(): got2 = lax.ppermute(second, axes, swap2)  2.82 us
    pallas_call x1, Pallas kernels, body(): pl.pallas_call(row_pack, grid=(1,), in_specs=[low3, high3] * 4 + [pl.Bloc...  2.09 us
    ppermute x1, starting transfers between devices, body(): got1 = lax.ppermute(first, axes, swap1)  2.02 us
    pallas_call x1, Pallas kernels, body(): pl.pallas_call(halo_rows, grid=(1,), in_specs=[fixed(message, cols)] * 4...  1.8 us
  transfers between devices with their start and end apart: 4, of which 2 were waited for; matrix products, arithmetic and copies ran while one was open for 0% of the time, Pallas kernels for 17%

profile of v3, /device:TPU:13, one launch (start us, length us, event | category | flops | bytes accessed | tf_op | source)
XLA Modules:
  0.0 43.4 jit_solution(544703376691610843)
XLA Ops:
  0.6 2.1 %row_pack.1 = (f32[88,256]{1,0:T(8,128)}, f32[88,256]{1,0:T(8,128)}) custom-call(f32[16,152,256]{2,1,0:T(8,128)} %t_hbm.1, f32[16,152,256]{2,1,0:T(8,128)} %t_hbm.1, f32[16,152,256]{2,1,0:T(8,128)} %s_hbm.1, f32[16,152,256]{2,1,0:T(8,128)} %s_hbm.1, f32[16,152,256]{2,1,0:T(8,128)} %u_hbm.1, f32[16,152,256]{2,1,0:T(8,128)} %u_hbm.1, f32[16,152,256]{2,1,0:T(8,128)} %v_hbm.1, ...), custom_call_target="tpu_custom_call" | custom-call | tf_op jit(solution)/shard_map/row_pack/pallas_call | solution.py:617
  2.7 2.0 %collective-permute-start = (f32[88,256]{1,0:T(8,128)}, f32[88,256]{1,0:T(8,128)}, u32[]{:S(2)}, u32[]{:S(2)}) collective-permute-start(f32[88,256]{1,0:T(8,128)} %get-tuple-element.11.mine1), channel_id=1, source_target_pairs={{0,1},{1,0},{2,3},{3,2},{4,5},{5,4},{6,7},{7,6},{8,9},{9,8},{10,11... | collective-permute-start | bytes 270344 | tf_op jit(solution)/shard_map/ppermute | solution.py:645
  4.7 2.8 %collective-permute-start.1 = (f32[88,256]{1,0:T(8,128)}, f32[88,256]{1,0:T(8,128)}, u32[]{:S(2)}, u32[]{:S(2)}) collective-permute-start(f32[88,256]{1,0:T(8,128)} %get-tuple-element.12.mine2), channel_id=1, source_target_pairs={{1,2},{2,1},{3,4},{4,3},{5,6},{6,5},{7,127},{0,0},{9,10},{10,9},{1... | collective-permute-start | bytes 270344 | tf_op jit(solution)/shard_map/ppermute | solution.py:646
  7.6 5.4 %column_pack.1 = (f32[160,128]{1,0:T(8,128)}, f32[160,128]{1,0:T(8,128)}) custom-call(f32[16,152,256]{2,1,0:T(8,128)} %t_hbm.1, f32[16,152,256]{2,1,0:T(8,128)} %s_hbm.1, f32[16,152,256]{2,1,0:T(8,128)} %u_hbm.1, f32[16,152,256]{2,1,0:T(8,128)} %v_hbm.1, f32[6,152,256]{2,1,0:T(8,128)} %e_hbm.1, s32[152,256]{1,0:T(8,128)} %n_hbm.1), custom_call_target="tpu_custom_call" | custom-call | flops 12451840 | bytes 9961472 | tf_op jit(solution)/shard_map/column_pack/pallas_call | solution.py:651
  13.0 0.0 collective-permute-done.got1.u1.v1
  13.0 0.0 collective-permute-done.1.got2.u2.v2
  13.0 1.6 %corners.1 = (f32[160,128]{1,0:T(8,128)}, f32[160,128]{1,0:T(8,128)}) custom-call(f32[88,256]{1,0:T(8,128)} %collective-permute-done.got1.u1.v1, f32[88,256]{1,0:T(8,128)} %collective-permute-done.1.got2.u2.v2, f32[88,256]{1,0:T(8,128)} %collective-permute-done.got1.u1.v1, ...), custom_call_target="tpu_custom_call", output_to_operand_aliasing={{0}: (5, {}), {1}: (6, {})} | custom-call | tf_op jit(solution)/shard_map/corners/pallas_call | solution.py:670
  14.6 4.1 %collective-permute-start.3 = (f32[160,128]{1,0:T(8,128)}, f32[160,128]{1,0:T(8,128)}, u32[]{:S(2)}, u32[]{:S(2)}) collective-permute-start(f32[160,128]{1,0:T(8,128)} %get-tuple-element.18), channel_id=1, source_target_pairs={{0,8},{8,16},{16,24},{24,32},{32,40},{40,48},{48,56},{56,64},{64,7... | collective-permute-start | bytes 245768 | tf_op jit(solution)/shard_map/ppermute | solution.py:681
  18.7 0.0 collective-permute-start.2
  18.7 1.8 %halo_rows.1 = (f32[88,256]{1,0:T(8,128)}, f32[64,256]{1,0:T(8,128)}) custom-call(f32[88,256]{1,0:T(8,128)} %get-tuple-element.11.mine1, f32[88,256]{1,0:T(8,128)} %get-tuple-element.12.mine2, f32[88,256]{1,0:T(8,128)} %collective-permute-done.got1.u1.v1, f32[88,256]{1,0:T(8,128)} %collective-permute-done.1.got2.u2.v2, s32[32,128]{1,0:T(8,128)} %bitcast.2), custom_call_target="tpu_custom_call" | custom-call | flops 2490368 | bytes 1245184 | tf_op jit(solution)/shard_map/halo_rows/pallas_call | solution.py:684
  20.5 0.4 collective-permute-done.3.from_west_hbm
  20.9 2.9 %collective-permute-done.2.from_east_hbm = f32[160,128]{1,0:T(8,128)} collective-permute-done((f32[160,128]{1,0:T(8,128)}, f32[160,128]{1,0:T(8,128)}, u32[]{:S(2)}, u32[]{:S(2)}) %collective-permute-start.2) | collective-permute-done | bytes 81952 | tf_op jit(solution)/shard_map/ppermute | solution.py:682
  23.8 19.6 %ocean_step.1 = (f32[16,152,256]{2,1,0:T(8,128)}, f32[16,152,256]{2,1,0:T(8,128)}, f32[16,152,256]{2,1,0:T(8,128)}) custom-call(f32[16,152,256]{2,1,0:T(8,128)} %t_hbm.1, f32[16,152,256]{2,1,0:T(8,128)} %s_hbm.1, f32[16,152,256]{2,1,0:T(8,128)} %u_hbm.1, f32[16,152,256]{2,1,0:T(8,128)} %v_hbm.1, f32[6,152,256]{2,1,0:T(8,128)} %e_hbm.1, ...), custom_call_target="tpu_custom_call" | custom-call | tf_op jit(solution)/shard_map/ocean_step/pallas_call | solution.py:699
Async XLA Ops:
  2.7 10.3 %collective-permute-start = (f32[88,256]{1,0:T(8,128)}, f32[88,256]{1,0:T(8,128)}, u32[]{:S(2)}, u32[]{:S(2)}) collective-permute-start(f32[88,256]{1,0:T(8,128)} %get-tuple-element.11.mine1), channel_id=1, source_target_pairs={{0,1},{1,0},{2,3},{3,2},{4,5},{5,4},{6,7},{7,6},{8,9},{9,8},{10,11... | collective-permute-start | bytes 270344 | tf_op jit(solution)/shard_map/ppermute | solution.py:645
  4.7 8.2 %collective-permute-start.1 = (f32[88,256]{1,0:T(8,128)}, f32[88,256]{1,0:T(8,128)}, u32[]{:S(2)}, u32[]{:S(2)}) collective-permute-start(f32[88,256]{1,0:T(8,128)} %get-tuple-element.12.mine2), channel_id=1, source_target_pairs={{1,2},{2,1},{3,4},{4,3},{5,6},{6,5},{7,127},{0,0},{9,10},{10,9},{1... | collective-permute-start | bytes 270344 | tf_op jit(solution)/shard_map/ppermute | solution.py:646
  14.6 6.3 %collective-permute-start.3 = (f32[160,128]{1,0:T(8,128)}, f32[160,128]{1,0:T(8,128)}, u32[]{:S(2)}, u32[]{:S(2)}) collective-permute-start(f32[160,128]{1,0:T(8,128)} %get-tuple-element.18), channel_id=1, source_target_pairs={{0,8},{8,16},{16,24},{24,32},{32,40},{40,48},{48,56},{56,64},{64,7... | collective-permute-start | bytes 245768 | tf_op jit(solution)/shard_map/ppermute | solution.py:681
  18.7 5.1 %collective-permute-start.2 = (f32[160,128]{1,0:T(8,128)}, f32[160,128]{1,0:T(8,128)}, u32[]{:S(2)}, u32[]{:S(2)}) collective-permute-start(f32[160,128]{1,0:T(8,128)} %get-tuple-element.17.own_hbm), channel_id=1, source_target_pairs={{8,0},{16,8},{24,16},{32,24},{40,32},{48,40},{56,48},{64,56},{72,6... | collective-permute-start | bytes 245768 | tf_op jit(solution)/shard_map/ppermute | solution.py:682

commit v4 on v2

--- a/solution.py
+++ b/solution.py
@@ -639,6 +639,7 @@
         for lat in range(1, lats - 1, 2):
             swap2 += [(place(lat, lon), place(lat + 1, lon)), (place(lat + 1, lon), place(lat, lon))]
         swap2.append((place(lats - 1, lon), place(lats - 1, lons - 1 - lon)))
+        swap2.append((place(0, lon), place(0, lons - 1 - lon)))
     got1 = lax.ppermute(first, axes, swap1)
     got2 = lax.ppermute(second, axes, swap2)
 

time: 43.6 us -> 43.9 us (level)
  the two profiles are of different devices: /device:TPU:13 before, /device:TPU:0 now
where the time goes in v4:
time: 43.9 us; the launch traced here: 43.7 us
  Pallas kernels  30.4 us (69%)
  starting transfers between devices  10.4 us (24%)
  waiting for transfers between devices  2.24 us (5%)
  between operations  0.64 us (1%)
    pallas_call x1, Pallas kernels, body(): pl.pallas_call(step_kernel, in_specs=[anywhere] * 12, out_specs=[anywhere...  19.5 us
    pallas_call x1, Pallas kernels, body(): pl.pallas_call(lambda *refs: column_pack(group, *refs), grid=(levels // g...  5.38 us
    ppermute x1, starting transfers between devices, body(): got2 = lax.ppermute(second, axes, swap2)  3.31 us
    ppermute x1, starting transfers between devices, body(): got1 = lax.ppermute(first, axes, swap1)  3.28 us
    ppermute x1, starting transfers between devices, body(): lax.ppermute(to_west, 'lon', [((i + 1) % lons, i) for i in range(lons)])  2.88 us
    pallas_call x1, Pallas kernels, body(): pl.pallas_call(row_pack, grid=(1,), in_specs=[low3, high3] * 4 + [pl.Bloc...  2.09 us
    pallas_call x1, Pallas kernels, body(): pl.pallas_call(halo_rows, grid=(1,), in_specs=[fixed(message, cols)] * 4...  1.8 us
    pallas_call x1, Pallas kernels, body(): pl.pallas_call(corners, grid=(1,), in_specs=[u_rows, u_rows, v_rows, v_ro...  1.6 us
  transfers between devices with their start and end apart: 4, of which 2 were waited for; matrix products, arithmetic and copies ran while one was open for 0% of the time, Pallas kernels for 16%

profile of v4, /device:TPU:0, one launch (start us, length us, event | category | flops | bytes accessed | tf_op | source)
XLA Modules:
  0.0 43.7 jit_solution(5030230451932981812)
XLA Ops:
  0.6 2.1 %row_pack.1 = (f32[88,256]{1,0:T(8,128)}, f32[88,256]{1,0:T(8,128)}) custom-call(f32[16,152,256]{2,1,0:T(8,128)} %t_hbm.1, f32[16,152,256]{2,1,0:T(8,128)} %t_hbm.1, f32[16,152,256]{2,1,0:T(8,128)} %s_hbm.1, f32[16,152,256]{2,1,0:T(8,128)} %s_hbm.1, f32[16,152,256]{2,1,0:T(8,128)} %u_hbm.1, f32[16,152,256]{2,1,0:T(8,128)} %u_hbm.1, f32[16,152,256]{2,1,0:T(8,128)} %v_hbm.1, ...), custom_call_target="tpu_custom_call" | custom-call | tf_op jit(solution)/shard_map/row_pack/pallas_call | solution.py:615
  2.7 3.3 %collective-permute-start = (f32[88,256]{1,0:T(8,128)}, f32[88,256]{1,0:T(8,128)}, u32[]{:S(2)}, u32[]{:S(2)}) collective-permute-start(f32[88,256]{1,0:T(8,128)} %get-tuple-element.11.mine1), channel_id=1, source_target_pairs={{0,1},{1,0},{2,3},{3,2},{4,5},{5,4},{6,7},{7,6},{8,9},{9,8},{10,11... | collective-permute-start | bytes 270344 | tf_op jit(solution)/shard_map/ppermute | solution.py:643
  6.0 3.3 %collective-permute-start.1 = (f32[88,256]{1,0:T(8,128)}, f32[88,256]{1,0:T(8,128)}, u32[]{:S(2)}, u32[]{:S(2)}) collective-permute-start(f32[88,256]{1,0:T(8,128)} %get-tuple-element.12.mine2), channel_id=1, source_target_pairs={{1,2},{2,1},{3,4},{4,3},{5,6},{6,5},{7,127},{0,120},{9,10},{10,9},... | collective-permute-start | bytes 270344 | tf_op jit(solution)/shard_map/ppermute | solution.py:644
  9.3 5.4 %column_pack.1 = (f32[160,128]{1,0:T(8,128)}, f32[160,128]{1,0:T(8,128)}) custom-call(f32[16,152,256]{2,1,0:T(8,128)} %t_hbm.1, f32[16,152,256]{2,1,0:T(8,128)} %s_hbm.1, f32[16,152,256]{2,1,0:T(8,128)} %u_hbm.1, f32[16,152,256]{2,1,0:T(8,128)} %v_hbm.1, f32[6,152,256]{2,1,0:T(8,128)} %e_hbm.1, s32[152,256]{1,0:T(8,128)} %n_hbm.1), custom_call_target="tpu_custom_call" | custom-call | flops 12451840 | bytes 9961472 | tf_op jit(solution)/shard_map/column_pack/pallas_call | solution.py:649
  14.7 0.0 collective-permute-done.got1.u1.v1
  14.7 0.8 %collective-permute-done.1.got2.u2.v2 = f32[88,256]{1,0:T(8,128)} collective-permute-done((f32[88,256]{1,0:T(8,128)}, f32[88,256]{1,0:T(8,128)}, u32[]{:S(2)}, u32[]{:S(2)}) %collective-permute-start.1) | collective-permute-done | bytes 90144 | tf_op jit(solution)/shard_map/ppermute | solution.py:644
  15.5 1.6 %corners.1 = (f32[160,128]{1,0:T(8,128)}, f32[160,128]{1,0:T(8,128)}) custom-call(f32[88,256]{1,0:T(8,128)} %collective-permute-done.got1.u1.v1, f32[88,256]{1,0:T(8,128)} %collective-permute-done.1.got2.u2.v2, f32[88,256]{1,0:T(8,128)} %collective-permute-done.got1.u1.v1, ...), custom_call_target="tpu_custom_call", output_to_operand_aliasing={{0}: (5, {}), {1}: (6, {})} | custom-call | tf_op jit(solution)/shard_map/corners/pallas_call | solution.py:668
  17.1 1.0 %collective-permute-start.3 = (f32[160,128]{1,0:T(8,128)}, f32[160,128]{1,0:T(8,128)}, u32[]{:S(2)}, u32[]{:S(2)}) collective-permute-start(f32[160,128]{1,0:T(8,128)} %get-tuple-element.18), channel_id=1, source_target_pairs={{0,8},{8,16},{16,24},{24,32},{32,40},{40,48},{48,56},{56,64},{64,7... | collective-permute-start | bytes 245768 | tf_op jit(solution)/shard_map/ppermute | solution.py:679
  18.1 2.9 %collective-permute-start.2 = (f32[160,128]{1,0:T(8,128)}, f32[160,128]{1,0:T(8,128)}, u32[]{:S(2)}, u32[]{:S(2)}) collective-permute-start(f32[160,128]{1,0:T(8,128)} %get-tuple-element.17.own_hbm), channel_id=1, source_target_pairs={{8,0},{16,8},{24,16},{32,24},{40,32},{48,40},{56,48},{64,56},{72,6... | collective-permute-start | bytes 245768 | tf_op jit(solution)/shard_map/ppermute | solution.py:680
  21.0 1.8 %halo_rows.1 = (f32[88,256]{1,0:T(8,128)}, f32[64,256]{1,0:T(8,128)}) custom-call(f32[88,256]{1,0:T(8,128)} %get-tuple-element.11.mine1, f32[88,256]{1,0:T(8,128)} %get-tuple-element.12.mine2, f32[88,256]{1,0:T(8,128)} %collective-permute-done.got1.u1.v1, f32[88,256]{1,0:T(8,128)} %collective-permute-done.1.got2.u2.v2, s32[32,128]{1,0:T(8,128)} %bitcast.2), custom_call_target="tpu_custom_call" | custom-call | flops 2490368 | bytes 1245184 | tf_op jit(solution)/shard_map/halo_rows/pallas_call | solution.py:682
  22.8 1.4 %collective-permute-done.3.from_west_hbm = f32[160,128]{1,0:T(8,128)} collective-permute-done((f32[160,128]{1,0:T(8,128)}, f32[160,128]{1,0:T(8,128)}, u32[]{:S(2)}, u32[]{:S(2)}) %collective-permute-start.3) | collective-permute-done | bytes 81952 | tf_op jit(solution)/shard_map/ppermute | solution.py:679
  24.2 0.0 collective-permute-done.2.from_east_hbm
  24.2 19.5 %ocean_step.1 = (f32[16,152,256]{2,1,0:T(8,128)}, f32[16,152,256]{2,1,0:T(8,128)}, f32[16,152,256]{2,1,0:T(8,128)}) custom-call(f32[16,152,256]{2,1,0:T(8,128)} %t_hbm.1, f32[16,152,256]{2,1,0:T(8,128)} %s_hbm.1, f32[16,152,256]{2,1,0:T(8,128)} %u_hbm.1, f32[16,152,256]{2,1,0:T(8,128)} %v_hbm.1, f32[6,152,256]{2,1,0:T(8,128)} %e_hbm.1, ...), custom_call_target="tpu_custom_call" | custom-call | tf_op jit(solution)/shard_map/ocean_step/pallas_call | solution.py:697
Async XLA Ops:
  2.7 12.0 %collective-permute-start = (f32[88,256]{1,0:T(8,128)}, f32[88,256]{1,0:T(8,128)}, u32[]{:S(2)}, u32[]{:S(2)}) collective-permute-start(f32[88,256]{1,0:T(8,128)} %get-tuple-element.11.mine1), channel_id=1, source_target_pairs={{0,1},{1,0},{2,3},{3,2},{4,5},{5,4},{6,7},{7,6},{8,9},{9,8},{10,11... | collective-permute-start | bytes 270344 | tf_op jit(solution)/shard_map/ppermute | solution.py:643
  6.0 9.5 %collective-permute-start.1 = (f32[88,256]{1,0:T(8,128)}, f32[88,256]{1,0:T(8,128)}, u32[]{:S(2)}, u32[]{:S(2)}) collective-permute-start(f32[88,256]{1,0:T(8,128)} %get-tuple-element.12.mine2), channel_id=1, source_target_pairs={{1,2},{2,1},{3,4},{4,3},{5,6},{6,5},{7,127},{0,120},{9,10},{10,9},... | collective-permute-start | bytes 270344 | tf_op jit(solution)/shard_map/ppermute | solution.py:644
  17.1 7.1 %collective-permute-start.3 = (f32[160,128]{1,0:T(8,128)}, f32[160,128]{1,0:T(8,128)}, u32[]{:S(2)}, u32[]{:S(2)}) collective-permute-start(f32[160,128]{1,0:T(8,128)} %get-tuple-element.18), channel_id=1, source_target_pairs={{0,8},{8,16},{16,24},{24,32},{32,40},{40,48},{48,56},{56,64},{64,7... | collective-permute-start | bytes 245768 | tf_op jit(solution)/shard_map/ppermute | solution.py:679
  18.1 6.1 %collective-permute-start.2 = (f32[160,128]{1,0:T(8,128)}, f32[160,128]{1,0:T(8,128)}, u32[]{:S(2)}, u32[]{:S(2)}) collective-permute-start(f32[160,128]{1,0:T(8,128)} %get-tuple-element.17.own_hbm), channel_id=1, source_target_pairs={{8,0},{16,8},{24,16},{32,24},{40,32},{48,40},{56,48},{64,56},{72,6... | collective-permute-start | bytes 245768 | tf_op jit(solution)/shard_map/ppermute | solution.py:680
